TPU v7x, 256 devices: a whole 4x4x8 slice. The times are simulated.
256 devices in a mesh: blk: 8 (over x, core), cond: 32 (over z, y).
Axes of the slice: x: 4, y: 4, z: 8, core: 2. Of those that a mesh axis runs over, the one named last changes fastest.
Arguments:
- adjoint_in: float32 [32, 6, 256, 8, 128], P('cond', None, 'blk'), may hold values from -6 to 6
- source: float32 [32, 6, 256, 8, 128], P('cond', None, 'blk'), may hold values from -6 to 6
- second_coef: float32 [32, 256, 8, 128], P('cond', 'blk'), may hold values from 0.05 to 0.5
- fourth_coef: float32 [32, 256, 8, 128], P('cond', 'blk'), may hold values from 0.02 to 0.08
- time_step: float32 [32, 256, 8, 128], P('cond', 'blk'), may hold values from 0.08 to 0.25
- jacobians: float32 [32, 2, 6, 6], P('cond'), may hold values from -2.5 to 2.5
- cond_weight: float32 [32], P('cond'), may hold values from 0.05 to 0.2
- wall_grad: float32 [32, 6, 256, 128], P('cond', None, 'blk'), may hold values from -6 to 6
- wall_mask: int32 [256, 128], P('blk'), may hold values 0 or 1
- face_perm: int32 [8, 2, 128, 128], P('blk'), may hold values from 0 to 1, as said below
- lengths: int32 [8], P('blk'), may hold values from 8 to 32, as said below
Outputs:
- adjoint_out: float32 [32, 6, 256, 8, 128], P('cond', None, 'blk')
- sensitivity: float32 [256, 128], P('blk')
Inputs may be any that keep to these rules, and one draw needn't show every extreme that they name: face_perm[b, 0] and face_perm[b, 1] have exactly one 1 in each row and column; face_perm[b, 1] is the transpose of face_perm[b + 1, 0], blocks taken around the loop. `lengths`: at least one block has exactly 32 active cells.
All inputs are finite; a program needn't handle non-finite values. No bound on the sum of `wall_mask` on one device may be relied on, other than what follows from the above.
Results may differ from a plain program's by a relative error of at most 0.0001.
Values sent between devices are 32-bit elements; how exact they have to be, the bound alone decides.
No kernel may reach another device: no remote copies, remote signals or barrier semaphores. Data moves between devices by JAX's collectives and lax.ppermute only.
A program may use at most 64 MiB of HBM per device.

v0:
```python
import functools

import jax
import jax.numpy as jnp
from jax import lax
from jax.experimental import pallas as pl
from jax.experimental.pallas import tpu as pltpu
from jax.sharding import PartitionSpec as P

NV = 6
SLOTS = 32
J = 8
K = 128
DEEP = 6
NEAR = 4
EXT = SLOTS + 2 * DEEP
PLANES = NV * DEEP + 2 * DEEP + NV * NEAR + NEAR
FACTORS = (0.6, 0.6, 1.0)
GROUP = 8
ROWS = NV * J

VMEM = pl.BlockSpec(memory_space=pltpu.VMEM)
SMEM = pl.BlockSpec(memory_space=pltpu.SMEM)
HBM = pl.BlockSpec(memory_space=pl.ANY)
PARAMS = pltpu.CompilerParams(vmem_limit_bytes=32 * 1024 * 1024)


def odd_place():
    return lax.rem(lax.axis_index("blk"), 2) == 1


def message_spans():
    at = 0
    for name, fields, depth in (("state", NV, DEEP), ("second", 1, DEEP), ("fourth", 1, DEEP), ("source", NV, NEAR), ("step", 1, NEAR)):
        for field in range(fields):
            yield name, field if fields > 1 else None, at, depth
            at += depth


def pack_kernel(lengths, state, source, second, fourth, step, on_send, cross_send, sem):
    refs = {"state": state, "source": source, "second": second, "fourth": fourth, "step": step}
    odd = odd_place()

    def start_copies(out, out_sem, tail):
        for name, field, at, depth in message_spans():
            ref = refs[name].at[0] if field is None else refs[name].at[0, field]
            first = lengths[0] - depth if tail else 0
            pltpu.make_async_copy(ref.at[pl.ds(first, depth)], out.at[pl.ds(at, depth)], out_sem).start()

    @pl.when(odd)
    def _():
        start_copies(on_send, sem.at[0], False)

    @pl.when(jnp.logical_not(odd))
    def _():
        start_copies(cross_send, sem.at[1], False)

    @pl.when(odd)
    def _():
        start_copies(cross_send, sem.at[1], True)

    @pl.when(jnp.logical_not(odd))
    def _():
        start_copies(on_send, sem.at[0], True)

    pltpu.make_async_copy(on_send, on_send, sem.at[0]).wait()
    pltpu.make_async_copy(cross_send, cross_send, sem.at[1]).wait()


def edge_rows():
    row = lax.broadcasted_iota(jnp.int32, (J, K), 0)
    return row == J - 1, row == 0


def shift_up(values):
    return pltpu.roll(values, J - 1, 0)


def shift_down(values):
    return pltpu.roll(values, 1, 0)


def two_parts(values):
    high = values.astype(jnp.bfloat16)
    return high, (values - high.astype(jnp.float32)).astype(jnp.bfloat16)


def flux_matrix(jac):
    width = 4 * ROWS
    lane = lax.broadcasted_iota(jnp.int32, (J, width), 1)
    row = lax.broadcasted_iota(jnp.int32, (J, width), 0)
    lane = jnp.where(lane >= 2 * ROWS, lane - 2 * ROWS, lane)
    pair = lane // J
    j = lane % J
    pattern = jnp.where(pair < NV, (j == row).astype(jnp.float32), (j == row + 1).astype(jnp.float32) - (j == row - 1).astype(jnp.float32))
    blocks = []
    for v in range(NV):
        block = jnp.zeros((J, width), jnp.float32)
        for axis in range(2):
            for u in range(NV):
                block = jnp.where(pair == axis * NV + u, -0.5 * jac[0, axis, u, v], block)
        blocks.append(block * pattern)
    high, low = two_parts(jnp.concatenate(blocks, 0))
    return jnp.concatenate([high, low], 0)


def flux_terms(matrix, state, cells):
    columns = []
    for e in cells:
        along = (state[:, e + 1] - state[:, e - 1]).reshape(ROWS, K)
        here = state[:, e].reshape(ROWS, K)
        high, low = two_parts(jnp.concatenate([along, here], 0))
        columns.append(jnp.concatenate([high, low], 0))
    product = jnp.dot(matrix, jnp.concatenate(columns, 1), preferred_element_type=jnp.float32)
    product = product[:ROWS] + product[ROWS:]
    return [[product[v * J : (v + 1) * J, n * K : (n + 1) * K] for v in range(NV)] for n in range(len(cells))]


def advance(factor, matrix, runs, anchor, state, result, fields):
    source, second, fourth, step = fields
    top, bottom = edge_rows()
    flux = flux_terms(matrix, state, [first + n for first, count in runs for n in range(count)])
    for first, count in runs:
        s2 = [second[first + n] for n in range(-1, count + 1)]
        s4 = [fourth[first + n] for n in range(-2, count + 2)]
        side = [a + 4.0 * b for a, b in zip(s2, s4[1:])]
        centre = [4.0 * a + 6.0 * b for a, b in zip(s2[1:], s4[2:])][:count]
        above = [jnp.where(top, 0.0, shift_up(a)) for a in s2[1 : count + 1]]
        below = [jnp.where(bottom, 0.0, shift_down(a)) for a in s2[1 : count + 1]]
        scale = [factor * step[first + n] for n in range(count)]
        for v in range(NV):
            p = [state[v, first + n] for n in range(-2, count + 2)]
            r = [a * b for a, b in zip(side, p[1:])]
            q = [a * b for a, b in zip(s4, p)]
            for n in range(count):
                here = p[n + 2]
                change = (
                    flux[n][v]
                    + centre[n] * here
                    - (r[n] + r[n + 2])
                    + (q[n] + q[n + 4])
                    - (above[n] * shift_up(here) + below[n] * shift_down(here))
                    + source[v, first + n]
                )
                result[v, first + n] = anchor[v, first + n] - scale[n] * change
        flux = flux[count:]


def interior(active_len, matrix, states, fields):
    anchor = states[0]
    for s in range(3):
        lead = 2 * (s + 1)
        groups = lax.div(jnp.maximum(active_len - 2 * lead, 0) + (GROUP - 1), GROUP)

        def step(g, _, s=s, lead=lead):
            first = DEEP + lead + g * GROUP
            advance(FACTORS[s], matrix[...], [(first, GROUP)], anchor, states[s], states[s + 1], fields)
            return 0

        lax.fori_loop(0, groups, step, 0)


def boundary(active_len, matrix, states, fields):
    anchor = states[0]
    for s in range(3):
        lead = 2 * (s + 1)
        runs = [(lead, DEEP), (active_len + DEEP - lead, DEEP)]
        advance(FACTORS[s], matrix[...], runs, anchor, states[s], states[s + 1], fields)


def span_index(perm):
    marks = lax.broadcasted_iota(jnp.int32, (J, K), 1).astype(jnp.bfloat16)
    one_hot = perm.astype(jnp.float32).astype(jnp.bfloat16)
    found = lax.dot_general(marks, one_hot, (((1,), (1,)), ((), ())), preferred_element_type=jnp.float32)
    return found.astype(jnp.int32)


def take_span(values, index):
    return jnp.take_along_axis(values, index, axis=1, mode="promise_in_bounds")


def sides(active_len, on, cross):
    odd = odd_place()
    return ((odd, on), (jnp.logical_not(odd), cross))


def first_interior_kernel(
    lengths, jac, perm, state_in, source_in, second_in, fourth_in, step_in,
    index, matrix, state, source, second, fourth, step, one, two, three,
    sem,
):
    body = pl.ds(DEEP, SLOTS)
    copies = [
        pltpu.make_async_copy(state_in.at[0], state.at[:, body], sem.at[0]),
        pltpu.make_async_copy(second_in.at[0], second.at[body], sem.at[1]),
        pltpu.make_async_copy(fourth_in.at[0], fourth.at[body], sem.at[2]),
        pltpu.make_async_copy(source_in.at[0], source.at[:, body], sem.at[3]),
        pltpu.make_async_copy(step_in.at[0], step.at[body], sem.at[4]),
    ]
    for copy in copies:
        copy.start()
    for side in range(2):
        index[side] = span_index(perm[0, side])
    matrix[...] = flux_matrix(jac)
    for copy in copies:
        copy.wait()
    interior(lengths[0], matrix, (state, one, two, three), (source, second, fourth, step))


def first_boundary_kernel(
    lengths, index, matrix, on_got, cross_got, state_in, source_in, second_in, fourth_in, step_in, one_in, two_in, three_in,
    state, source, second, fourth, step, one, two, three, on_send, cross_send,
):
    active_len = lengths[0]
    refs = {"state": state, "source": source, "second": second, "fourth": fourth, "step": step}
    for before, got in sides(active_len, on_got, cross_got):
        perm = jnp.where(before, index[0], index[1])
        for name, field, at, depth in message_spans():
            ref = refs[name] if field is None else refs[name].at[field]
            base = jnp.where(before, DEEP - depth, active_len + DEEP)
            for layer in range(depth):
                ref[base + layer] = take_span(got[at + layer], perm)
    boundary(active_len, matrix, (state, one, two, three), (source, second, fourth, step))
    for lead, out in sides(active_len, on_send, cross_send):
        base = jnp.where(lead, DEEP, active_len)
        for v in range(NV):
            for layer in range(DEEP):
                out[v * DEEP + layer] = three[v, base + layer]


def second_interior_kernel(
    lengths, matrix, state, source, second, fourth, step, wall_grad,
    one, two, three, wall_start, wall,
):
    active_len = lengths[0]
    interior(active_len, matrix, (state, one, two, three), (source, second, fourth, step))
    body = pl.ds(DEEP, SLOTS)
    start = jnp.zeros((SLOTS, K), jnp.float32)
    more = jnp.zeros((SLOTS, K), jnp.float32)
    for v in range(NV):
        start = start + state[v, body, 0, :] * wall_grad[0, v]
        more = more + three[v, body, 0, :] * wall_grad[0, v]
    slot = lax.broadcasted_iota(jnp.int32, (SLOTS, K), 0)
    wall_start[...] = start
    wall[...] = jnp.where((slot >= DEEP) & (slot < active_len - DEEP), start + more, 0.0)


def second_boundary_kernel(
    lengths, weight, index, matrix, on_got, cross_got, source, second, fourth, step, wall_grad, wall_mask, wall_start, wall_in,
    state_in, one_in, two_in, three_in,
    state, one, two, three, wall,
    rows,
):
    active_len = lengths[0]
    for before, got in sides(active_len, on_got, cross_got):
        perm = jnp.where(before, index[0], index[1])
        base = jnp.where(before, 0, active_len + DEEP)
        for v in range(NV):
            for layer in range(DEEP):
                state[v, base + layer] = take_span(got[v * DEEP + layer], perm)
    boundary(active_len, matrix, (state, one, two, three), (source, second, fourth, step))
    rows[...] = wall_in[...]
    for base in (0, active_len - DEEP):
        for layer in range(DEEP):
            slot = pl.ds(base + layer, 1)
            total = wall_start[slot]
            for v in range(NV):
                total = total + three[v, base + layer + DEEP, pl.ds(0, 1), :] * wall_grad[0, v, slot]
            rows[slot] = total
    wall[...] = rows[...] * weight[0] * wall_mask[...].astype(jnp.float32)


def f32(*shape):
    return jax.ShapeDtypeStruct(shape, jnp.float32)


def call(kernel, name, outs, ins, out_specs=None, scratch=(), aliases=None):
    return pl.pallas_call(
        kernel, name=name, out_shape=outs, in_specs=ins, out_specs=out_specs or [VMEM] * len(outs),
        scratch_shapes=list(scratch), input_output_aliases=aliases or {}, compiler_params=PARAMS,
    )


def sum_over_conditions(value, z_size, y_size):
    pairs = [(z * y_size + y, (z ^ 1) * y_size + y) for z in range(z_size) for y in range(y_size)]
    groups = [[z * y_size + y for z in range(half, z_size, 2) for y in range(y_size)] for half in range(2)]
    value = value + lax.ppermute(value, "cond", pairs)
    copies = jnp.broadcast_to(value[None], (len(groups[0]),) + value.shape)
    return lax.all_to_all(copies, "cond", 0, 0, tiled=True, axis_index_groups=groups).sum(0)


def body(blocks, z_size, y_size, adjoint_in, source, second_coef, fourth_coef, time_step, jacobians, cond_weight, wall_grad,
         wall_mask, face_perm, lengths):
    chip = [(b, b ^ 1) for b in range(blocks)]
    cross = [(b, (b + (1 if b % 2 else -1)) % blocks) for b in range(blocks)]

    def exchange(on_send, cross_send):
        cross_got = lax.ppermute(cross_send, "blk", cross)
        return lax.ppermute(on_send, "blk", chip), cross_got

    planes, plane = f32(NV, EXT, J, K), f32(EXT, J, K)
    inputs = [pltpu.with_memory_space_constraint(x, pltpu.HBM) for x in (adjoint_in, source, second_coef, fourth_coef, time_step)]
    on_send, cross_send = call(
        pack_kernel, "pack_rims", [f32(PLANES, J, K)] * 2, [SMEM] + [HBM] * 5, scratch=[pltpu.SemaphoreType.DMA((2,))],
    )(lengths, *inputs)
    on_got, cross_got = exchange(on_send, cross_send)
    index, matrix, *arrays = call(
        first_interior_kernel, "first_interior",
        [jax.ShapeDtypeStruct((2, J, K), jnp.int32), jax.ShapeDtypeStruct((2 * ROWS, 4 * ROWS), jnp.bfloat16), planes, planes,
         plane, plane, plane, planes, planes, planes],
        [SMEM, SMEM, VMEM] + [HBM] * 5, scratch=[pltpu.SemaphoreType.DMA((5,))],
    )(lengths, jacobians, face_perm, *inputs)
    _, source_x, second_x, fourth_x, step_x, _, _, three, on_send, cross_send = call(
        first_boundary_kernel, "first_boundary",
        [planes, planes, plane, plane, plane, planes, planes, planes] + [f32(NV * DEEP, J, K)] * 2,
        [SMEM] + [VMEM] * 12, aliases={5 + n: n for n in range(8)},
    )(lengths, index, matrix, on_got, cross_got, *arrays)
    fields = (source_x, second_x, fourth_x, step_x)
    on_got, cross_got = exchange(on_send, cross_send)
    four, five, six, wall_start, wall = call(
        second_interior_kernel, "second_interior", [planes] * 3 + [f32(SLOTS, K)] * 2, [SMEM] + [VMEM] * 7,
    )(lengths, matrix, three, *fields, wall_grad)
    _, _, _, six, wall = call(
        second_boundary_kernel, "second_boundary", [planes] * 4 + [f32(SLOTS, K)],
        [SMEM] * 2 + [VMEM] * 16, scratch=[pltpu.VMEM((SLOTS, K), jnp.float32)], aliases={14 + n: n for n in range(4)},
    )(lengths, cond_weight, index, matrix, on_got, cross_got, *fields, wall_grad, wall_mask, wall_start, wall, three, four, five, six)
    active = lax.iota(jnp.int32, SLOTS) < lengths[0]
    adjoint = jnp.where(active[None, None, :, None, None], six[None, :, DEEP : DEEP + SLOTS], 0.0)
    return adjoint, sum_over_conditions(wall, z_size, y_size)


def solution(mesh):
    y_size = 4
    return jax.shard_map(
        functools.partial(body, mesh.shape["blk"], mesh.shape["cond"] // y_size, y_size),
        mesh=mesh,
        in_specs=(
            P("cond", None, "blk", None, None),
            P("cond", None, "blk", None, None),
            P("cond", "blk", None, None),
            P("cond", "blk", None, None),
            P("cond", "blk", None, None),
            P("cond", None, None, None),
            P("cond"),
            P("cond", None, "blk", None),
            P("blk", None),
            P("blk", None, None, None),
            P("blk"),
        ),
        out_specs=(P("cond", None, "blk", None, None), P("blk", None)),
        check_vma=False,
    )
```

profile of v0, /device:TPU:6, one launch (start us, length us, event | category | flops | bytes accessed | tf_op | source)
XLA Modules:
  0.0 47.1 jit_solution(5519661177800471560)
XLA Ops:
  0.6 0.0 copy-start.3
  0.6 0.0 copy-start.1
  1.3 1.1 %pack_rims.1 = (f32[76,8,128]{2,1,0:T(8,128)S(1)}, f32[76,8,128]{2,1,0:T(8,128)S(1)}) custom-call(s32[1]{0:T(128)} %copy.40.lengths, f32[1,6,32,8,128]{4,3,2,1,0:T(8,128)} %state.1, f32[1,6,32,8,128]{4,3,2,1,0:T(8,128)} %source.1, f32[1,32,8,128]{3,2,1,0:T(8,128)} %second.1, f32[1,32,8,128]{3,2,1,0:T(8,128)} %fourth.1, f32[1,32,8,128]{3,2,1,0:T(8,128)} %step.1), custom_call_target="tpu_custom_call" | custom-call | tf_op jit(solution)/shard_map/pack_rims/pallas_call | solution.py:303
  2.4 0.1 collective-permute-start
  2.5 0.9 %collective-permute-start.1 = (f32[76,8,128]{2,1,0:T(8,128)S(1)}, f32[76,8,128]{2,1,0:T(8,128)S(1)}, u32[]{:S(2)}, u32[]{:S(2)}) collective-permute-start(f32[76,8,128]{2,1,0:T(8,128)S(1)} %get-tuple-element.31), channel_id=1, source_target_pairs={{0,224},{32,64},{64,32},{96,128},{128,96},{160,192},{192,160},{224... | collective-permute-start | bytes 933896 | tf_op jit(solution)/shard_map/ppermute | solution.py:298
  3.4 0.0 copy-done.3
  3.4 0.0 copy-done.1
  3.4 4.3 %first_interior.1 = (s32[2,8,128]{2,1,0:T(8,128)S(1)}, bf16[96,192]{1,0:T(8,128)(2,1)S(1)}, f32[6,44,8,128]{3,2,1,0:T(8,128)S(1)}, f32[6,44,8,128]{3,2,1,0:T(8,1...) custom-call(s32[1]{0:T(128)} %copy.40.lengths, ...), custom_call_target="tpu_custom_call" | custom-call | tf_op jit(solution)/shard_map/first_interior/pallas_call | solution.py:307
  7.7 0.0 collective-permute-done.on_got
  7.7 1.2 %collective-permute-done.1.cross_got = f32[76,8,128]{2,1,0:T(8,128)S(1)} collective-permute-done((f32[76,8,128]{2,1,0:T(8,128)S(1)}, f32[76,8,128]{2,1,0:T(8,128)S(1)}, u32[]{:S(2)}, u32[]{:S(2)}) %collective-permute-start.1) | collective-permute-done | bytes 311328 | tf_op jit(solution)/shard_map/ppermute | solution.py:298
  8.9 0.0 copy-start
  8.9 1.2 %first_boundary.1 = (f32[6,44,8,128]{3,2,1,0:T(8,128)S(1)}, f32[6,44,8,128]{3,2,1,0:T(8,128)S(1)}, f32[44,8,128]{2,1,0:T(8,128)S(1)}, f32[44,8,128]{2,1,0:T(8,12...) custom-call(s32[1]{0:T(128)} %copy.40.lengths, ...), custom_call_target="tpu_custom_call", output_to_operand_aliasing={{0}: (5, {}), {1}: (6, {}), {2}: (7, {}), {3}: (8, {}), {4}... | custom-call | tf_op jit(solution)/shard_map/first_boundary/pallas_call | solution.py:313
  10.1 1.7 %collective-permute-start.2 = (f32[36,8,128]{2,1,0:T(8,128)S(1)}, f32[36,8,128]{2,1,0:T(8,128)S(1)}, u32[]{:S(2)}, u32[]{:S(2)}) collective-permute-start(f32[36,8,128]{2,1,0:T(8,128)S(1)} %get-tuple-element.40), channel_id=1, source_target_pairs={{0,32},{32,0},{64,96},{96,64},{128,160},{160,128},{192,224},{224,1... | collective-permute-start | bytes 442376 | tf_op jit(solution)/shard_map/ppermute | solution.py:299
  11.8 0.0 collective-permute-start.3
  12.5 0.0 copy-done
  12.5 0.0 copy-start.2
  12.5 2.2 %second_interior.1 = (f32[6,44,8,128]{3,2,1,0:T(8,128)S(1)}, f32[6,44,8,128]{3,2,1,0:T(8,128)S(1)}, f32[6,44,8,128]{3,2,1,0:T(8,128)S(1)}, f32[32,128]{1,0:T(8,128)S(1)}, f32[32,128]{1,0:T(8,128)S(1)}) custom-call(s32[1]{0:T(128)} %copy.40.lengths, bf16[96,192]{1,0:T(8,128)(2,1)S(1)} %get-tuple-element.29.matrix, ...), custom_call_target="tpu_custom_call" | custom-call | tf_op jit(solution)/shard_map/second_interior/pallas_call | solution.py:320
  14.7 0.0 collective-permute-done.2.on_got
  14.7 1.7 %collective-permute-done.3.cross_got = f32[36,8,128]{2,1,0:T(8,128)S(1)} collective-permute-done((f32[36,8,128]{2,1,0:T(8,128)S(1)}, f32[36,8,128]{2,1,0:T(8,128)S(1)}, u32[]{:S(2)}, u32[]{:S(2)}) %collective-permute-start.3) | collective-permute-done | bytes 147488 | tf_op jit(solution)/shard_map/ppermute | solution.py:298
  16.4 0.0 copy-done.2
  16.4 1.2 %second_boundary.1 = (f32[6,44,8,128]{3,2,1,0:T(8,128)S(1)}, f32[6,44,8,128]{3,2,1,0:T(8,128)S(1)}, f32[6,44,8,128]{3,2,1,0:T(8,128)S(1)}, f32[6,44,8,128]{3,2,1,0:T(8,128)S(1)}, f32[32,128]{1,0:T(8,128)S(1)}) custom-call(s32[1]{0:T(128)} %copy.40.lengths, ...), custom_call_target="tpu_custom_call", output_to_operand_aliasing={{0}: (14, {}), {1}: (15, {}), {2}: (16, {}), {3}: (17, {})} | custom-call | tf_op jit(solution)/shard_map/second_boundary/pallas_call | solution.py:323
  17.6 2.0 %collective-permute-start.4 = (f32[32,128]{1,0:T(8,128)S(1)}, f32[32,128]{1,0:T(8,128)S(1)}, u32[]{:S(2)}, u32[]{:S(2)}) collective-permute-start(f32[32,128]{1,0:T(8,128)S(1)} %get-tuple-element.53), channel_id=1, source_target_pairs={{0,4},{1,5},{2,6},{3,7},{4,0},{5,1},{6,2},{7,3},{8,12},{9,13},{10,... | collective-permute-start | bytes 49160 | tf_op jit(solution)/shard_map/ppermute | solution.py:287
  19.6 1.8 %collective-permute-done.4 = f32[32,128]{1,0:T(8,128)S(1)} collective-permute-done((f32[32,128]{1,0:T(8,128)S(1)}, f32[32,128]{1,0:T(8,128)S(1)}, u32[]{:S(2)}, u32[]{:S(2)}) %collective-permute-start.4) | collective-permute-done | bytes 16416 | tf_op jit(solution)/shard_map/ppermute | solution.py:287
  21.4 0.7 %broadcast_in_dim.22 = f32[16,32,128]{2,1,0:T(8,128)} broadcast(f32[32,128]{1,0:T(8,128)S(1)} %add.3), dimensions={1,2} | broadcast | bytes 278528 | tf_op jit(solution)/shard_map/broadcast_in_dim | solution.py:288
  22.1 11.2 %all-to-all-start = ((f32[16,32,128]{2,1,0:T(8,128)}), f32[16,32,128]{2,1,0:T(8,128)S(1)}, u32[]{:S(2)}, u32[]{:S(2)}) async-start(f32[16,32,128]{2,1,0:T(8,128)} %broadcast_in_dim.22), calls=%async_computation | async-start | bytes 524288 | tf_op jit(solution)/shard_map/all_to_all | solution.py:289
  33.4 1.0 %select_bitcast_fusion = f32[1,6,32,8,128]{4,3,2,1,0:T(8,128)} fusion(f32[6,44,8,128]{3,2,1,0:T(8,128)S(1)} %get-tuple-element.52, pred[32]{0:T(512)(128)(4,1)S(1)} %iota_compare_fusion), kind=kLoop, calls=%fused_computation | loop fusion | flops 196608 | bytes 1572896 | tf_op jit(solution)/shard_map/jit(_where)/select_n | solution.py:328
  34.4 12.1 %all-to-all-done = f32[16,32,128]{2,1,0:T(8,128)S(1)} async-done(((f32[16,32,128]{2,1,0:T(8,128)}), f32[16,32,128]{2,1,0:T(8,128)S(1)}, u32[]{:S(2)}, u32[]{:S(2)}) %all-to-all-start) | async-done | bytes 262176 | tf_op jit(solution)/shard_map/all_to_all | solution.py:289
  46.4 0.6 %reduce_sum.9 = f32[32,128]{1,0:T(8,128)} reduce(f32[16,32,128]{2,1,0:T(8,128)S(1)} %all-to-all-done, f32[]{:T(128)} %constant.0.clone.1), dimensions={0}, to_apply=%region_0.1 | reduce | flops 61440 | bytes 278532 | tf_op jit(solution)/shard_map/reduce_sum | solution.py:289
  (3 shorter events, 0.0 us)
Async XLA Ops:
  0.6 2.8 %copy-start.3 = (f32[1,2,6,6]{3,1,2,0:T(2,128)S(1)}, f32[1,2,6,6]{3,1,2,0:T(2,128)}, u32[]{:S(2)}) copy-start(f32[1,2,6,6]{3,1,2,0:T(2,128)} %param.16) | copy-start | bytes 868
  0.6 2.8 %copy-start.1 = (s32[1,2,128,128]{3,2,1,0:T(8,128)S(1)}, s32[1,2,128,128]{3,2,1,0:T(8,128)}, u32[]{:S(2)}) copy-start(s32[1,2,128,128]{3,2,1,0:T(8,128)} %perm.1) | copy-start | bytes 393220
  2.4 5.3 %collective-permute-start = (f32[76,8,128]{2,1,0:T(8,128)S(1)}, f32[76,8,128]{2,1,0:T(8,128)S(1)}, u32[]{:S(2)}, u32[]{:S(2)}) collective-permute-start(f32[76,8,128]{2,1,0:T(8,128)S(1)} %get-tuple-element.30), channel_id=1, source_target_pairs={{0,32},{32,0},{64,96},{96,64},{128,160},{160,128},{192,224},{224,1... | collective-permute-start | bytes 933896 | tf_op jit(solution)/shard_map/ppermute | solution.py:299
  2.5 6.4 %collective-permute-start.1 = (f32[76,8,128]{2,1,0:T(8,128)S(1)}, f32[76,8,128]{2,1,0:T(8,128)S(1)}, u32[]{:S(2)}, u32[]{:S(2)}) collective-permute-start(f32[76,8,128]{2,1,0:T(8,128)S(1)} %get-tuple-element.31), channel_id=1, source_target_pairs={{0,224},{32,64},{64,32},{96,128},{128,96},{160,192},{192,160},{224... | collective-permute-start | bytes 933896 | tf_op jit(solution)/shard_map/ppermute | solution.py:298
  8.9 3.6 %copy-start = (f32[1,6,32,128]{3,2,1,0:T(8,128)S(1)}, f32[1,6,32,128]{3,2,1,0:T(8,128)}, u32[]{:S(2)}) copy-start(f32[1,6,32,128]{3,2,1,0:T(8,128)} %wall_grad.3) | copy-start | bytes 294916
  10.1 4.6 %collective-permute-start.2 = (f32[36,8,128]{2,1,0:T(8,128)S(1)}, f32[36,8,128]{2,1,0:T(8,128)S(1)}, u32[]{:S(2)}, u32[]{:S(2)}) collective-permute-start(f32[36,8,128]{2,1,0:T(8,128)S(1)} %get-tuple-element.40), channel_id=1, source_target_pairs={{0,32},{32,0},{64,96},{96,64},{128,160},{160,128},{192,224},{224,1... | collective-permute-start | bytes 442376 | tf_op jit(solution)/shard_map/ppermute | solution.py:299
  11.8 4.6 %collective-permute-start.3 = (f32[36,8,128]{2,1,0:T(8,128)S(1)}, f32[36,8,128]{2,1,0:T(8,128)S(1)}, u32[]{:S(2)}, u32[]{:S(2)}) collective-permute-start(f32[36,8,128]{2,1,0:T(8,128)S(1)} %get-tuple-element.41), channel_id=1, source_target_pairs={{0,224},{32,64},{64,32},{96,128},{128,96},{160,192},{192,160},{224... | collective-permute-start | bytes 442376 | tf_op jit(solution)/shard_map/ppermute | solution.py:298
  12.5 3.9 %copy-start.2 = (s32[32,128]{1,0:T(8,128)S(1)}, s32[32,128]{1,0:T(8,128)}, u32[]{:S(2)}) copy-start(s32[32,128]{1,0:T(8,128)} %wall_mask.1) | copy-start | bytes 49156
  17.6 3.8 %collective-permute-start.4 = (f32[32,128]{1,0:T(8,128)S(1)}, f32[32,128]{1,0:T(8,128)S(1)}, u32[]{:S(2)}, u32[]{:S(2)}) collective-permute-start(f32[32,128]{1,0:T(8,128)S(1)} %get-tuple-element.53), channel_id=1, source_target_pairs={{0,4},{1,5},{2,6},{3,7},{4,0},{5,1},{6,2},{7,3},{8,12},{9,13},{10,... | collective-permute-start | bytes 49160 | tf_op jit(solution)/shard_map/ppermute | solution.py:287
  22.1 24.3 %all-to-all-start = ((f32[16,32,128]{2,1,0:T(8,128)}), f32[16,32,128]{2,1,0:T(8,128)S(1)}, u32[]{:S(2)}, u32[]{:S(2)}) async-start(f32[16,32,128]{2,1,0:T(8,128)} %broadcast_in_dim.22), calls=%async_computation | async-start | bytes 524288 | tf_op jit(solution)/shard_map/all_to_all | solution.py:289
where the time goes:
time: 47.4 us; the launch traced here: 47.1 us
  waiting for transfers between devices  16.8 us (35%)
  starting transfers between devices  16 us (34%)
  Pallas kernels  9.87 us (21%)
  between operations  2.08 us (4%)
  other arithmetic  1.64 us (3%)
  local copies, waits for them, and re-layouts  0.74 us (2%)
    all_to_all x1, waiting for transfers between devices, sum_over_conditions(): lax.all_to_all(copies, 'cond', 0, 0, tiled=True, axis_index_groups=groups)  12.1 us
    all_to_all x1, starting transfers between devices, sum_over_conditions(): lax.all_to_all(copies, 'cond', 0, 0, tiled=True, axis_index_groups=groups)  11.2 us
    pallas_call x1, Pallas kernels, body(): call(first_interior_kernel, 'first_interior', [jax.ShapeDtypeStruct((2, J...  4.26 us
    ppermute x2, waiting for transfers between devices, exchange(): cross_got = lax.ppermute(cross_send, 'blk', cross)  2.88 us
    pallas_call x1, Pallas kernels, body(): call(second_interior_kernel, 'second_interior', [planes] * 3 + [f32(SLOTS...  2.18 us
    ppermute x1, starting transfers between devices, sum_over_conditions(): value = value + lax.ppermute(value, 'cond', pairs)  2.01 us
    ppermute x1, waiting for transfers between devices, sum_over_conditions(): value = value + lax.ppermute(value, 'cond', pairs)  1.82 us
    ppermute x2, starting transfers between devices, exchange(): return (lax.ppermute(on_send, 'blk', chip), cross_got)  1.81 us
  transfers between devices with their start and end apart: 6, of which 4 were waited for; matrix products, arithmetic and copies ran while one was open for 2% of the time, Pallas kernels for 14%

commit v1 on v0

--- a/solution.py
+++ b/solution.py
@@ -281,12 +281,25 @@
     )
 
 
-def sum_over_conditions(value, z_size, y_size):
-    pairs = [(z * y_size + y, (z ^ 1) * y_size + y) for z in range(z_size) for y in range(y_size)]
-    groups = [[z * y_size + y for z in range(half, z_size, 2) for y in range(y_size)] for half in range(2)]
-    value = value + lax.ppermute(value, "cond", pairs)
-    copies = jnp.broadcast_to(value[None], (len(groups[0]),) + value.shape)
-    return lax.all_to_all(copies, "cond", 0, 0, tiled=True, axis_index_groups=groups).sum(0)
+def sum_over_conditions(value, adjoint, z_size, y_size):
+    def pairs(z_to, y_to):
+        return [(z * y_size + y, z_to(z) % z_size * y_size + y_to(y) % y_size) for z in range(z_size) for y in range(y_size)]
+
+    def same(n):
+        return n
+
+    def move(value, z_to, y_to):
+        return lax.ppermute(value, "cond", pairs(z_to, y_to))
+
+    def gather_sum(value, groups):
+        copies = jnp.broadcast_to(value[None], (len(groups[0]),) + value.shape)
+        return lax.all_to_all(copies, "cond", 0, 0, tiled=True, axis_index_groups=groups).sum(0)
+
+    value = value + move(value, lambda z: z ^ 1, same) + move(value, lambda z: z ^ 2, same) + move(value, lambda z: z ^ 3, same)
+    value, adjoint = lax.optimization_barrier((value, adjoint))
+    value = value + move(value, same, lambda y: y ^ 1) + move(value, same, lambda y: y ^ 2) + move(value, same, lambda y: y ^ 3)
+    value = value + move(value, lambda z: 7 - z, same)
+    return adjoint, value
 
 
 def body(blocks, z_size, y_size, adjoint_in, source, second_coef, fourth_coef, time_step, jacobians, cond_weight, wall_grad,
@@ -326,7 +339,7 @@
     )(lengths, cond_weight, index, matrix, on_got, cross_got, *fields, wall_grad, wall_mask, wall_start, wall, three, four, five, six)
     active = lax.iota(jnp.int32, SLOTS) < lengths[0]
     adjoint = jnp.where(active[None, None, :, None, None], six[None, :, DEEP : DEEP + SLOTS], 0.0)
-    return adjoint, sum_over_conditions(wall, z_size, y_size)
+    return sum_over_conditions(wall, adjoint, z_size, y_size)
 
 
 def solution(mesh):

time: 47.4 us -> 43.6 us (0.920)
  Pallas kernels: 9.87 us -> 7.87 us
  waiting for transfers between devices: 16.8 us -> 16 us
  local copies, waits for them, and re-layouts: 0.74 us -> 0.02 us
    all_to_all x1 -> x0, waiting for transfers between devices: 12.1 us -> none  [sum_over_conditions(): lax.all_to_all(copies, 'cond', 0, 0, tiled=True, axis_index_groups=groups)]
    all_to_all x1 -> x0, starting transfers between devices: 11.2 us -> none  [sum_over_conditions(): lax.all_to_all(copies, 'cond', 0, 0, tiled=True, axis_index_groups=groups)]
    ppermute x1 -> x7, starting transfers between devices: 2.01 us -> 13.1 us  [move(): return lax.ppermute(value, 'cond', pairs(z_to, y_to))]
    ppermute x1 -> x7, waiting for transfers between devices: 1.82 us -> 11.1 us  [move(): return lax.ppermute(value, 'cond', pairs(z_to, y_to))]
    ppermute x2, waiting for transfers between devices: 2.88 us -> 4.91 us  [exchange(): cross_got = lax.ppermute(cross_send, 'blk', cross)]
    pallas_call x1, Pallas kernels: 2.18 us -> 1.16 us  [body(): call(second_interior_kernel, 'second_interior', [planes] * 3 + [f32(SLOTS...]
    pallas_call x1, Pallas kernels: 4.26 us -> 3.24 us  [body(): call(first_interior_kernel, 'first_interior', [jax.ShapeDtypeStruct((2, J...]
    broadcast_in_dim x1 -> x0, local copies, waits for them, and re-layouts: 0.72 us -> none  [sum_over_conditions(): copies = jnp.broadcast_to(value[None], (len(groups[0]),) + value.shape)]
  transfers between devices with their start and end apart: 6 -> 11, of which waited for: 4 -> 7; matrix products, arithmetic and copies ran while one was open for 2% -> 2% of each run, Pallas kernels for 14% -> 10%
where the time goes in v1:
time: 43.6 us; the launch traced here: 43.4 us
  waiting for transfers between devices  16 us (37%)
  starting transfers between devices  15.8 us (36%)
  Pallas kernels  7.87 us (18%)
  between operations  2.07 us (5%)
  other arithmetic  1.63 us (4%)
    ppermute x7, starting transfers between devices, move(): return lax.ppermute(value, 'cond', pairs(z_to, y_to))  13.1 us
    ppermute x7, waiting for transfers between devices, move(): return lax.ppermute(value, 'cond', pairs(z_to, y_to))  11.1 us
    ppermute x2, waiting for transfers between devices, exchange(): cross_got = lax.ppermute(cross_send, 'blk', cross)  4.91 us
    pallas_call x1, Pallas kernels, body(): call(first_interior_kernel, 'first_interior', [jax.ShapeDtypeStruct((2, J...  3.24 us
    ppermute x2, starting transfers between devices, exchange(): return (lax.ppermute(on_send, 'blk', chip), cross_got)  1.79 us
    pallas_call x1, Pallas kernels, body(): call(second_boundary_kernel, 'second_boundary', [planes] * 4 + [f32(SLOTS...  1.22 us
    pallas_call x1, Pallas kernels, body(): call(first_boundary_kernel, 'first_boundary', [planes, planes, plane, pla...  1.2 us
    pallas_call x1, Pallas kernels, body(): call(second_interior_kernel, 'second_interior', [planes] * 3 + [f32(SLOTS...  1.16 us
  transfers between devices with their start and end apart: 11, of which 7 were waited for; matrix products, arithmetic and copies ran while one was open for 2% of the time, Pallas kernels for 10%

profile of v1, /device:TPU:6, one launch (start us, length us, event | category | flops | bytes accessed | tf_op | source)
XLA Modules:
  0.0 43.4 jit_solution(15784623606157913058)
XLA Ops:
  0.6 0.0 copy-start.3
  0.6 0.0 copy-start.1
  1.3 1.1 %pack_rims.1 = (f32[76,8,128]{2,1,0:T(8,128)S(1)}, f32[76,8,128]{2,1,0:T(8,128)S(1)}) custom-call(s32[1]{0:T(128)} %copy.39.lengths, f32[1,6,32,8,128]{4,3,2,1,0:T(8,128)} %state.1, f32[1,6,32,8,128]{4,3,2,1,0:T(8,128)} %source.1, f32[1,32,8,128]{3,2,1,0:T(8,128)} %second.1, f32[1,32,8,128]{3,2,1,0:T(8,128)} %fourth.1, f32[1,32,8,128]{3,2,1,0:T(8,128)} %step.1), custom_call_target="tpu_custom_call" | custom-call | tf_op jit(solution)/shard_map/pack_rims/pallas_call | solution.py:316
  2.4 0.1 collective-permute-start
  2.5 0.9 %collective-permute-start.1 = (f32[76,8,128]{2,1,0:T(8,128)S(1)}, f32[76,8,128]{2,1,0:T(8,128)S(1)}, u32[]{:S(2)}, u32[]{:S(2)}) collective-permute-start(f32[76,8,128]{2,1,0:T(8,128)S(1)} %get-tuple-element.33), channel_id=1, source_target_pairs={{0,224},{32,64},{64,32},{96,128},{128,96},{160,192},{192,160},{224... | collective-permute-start | bytes 933896 | tf_op jit(solution)/shard_map/ppermute | solution.py:311
  3.4 0.0 copy-done.3
  3.4 0.0 copy-done.1
  3.4 3.2 %first_interior.1 = (s32[2,8,128]{2,1,0:T(8,128)S(1)}, bf16[96,192]{1,0:T(8,128)(2,1)S(1)}, f32[6,44,8,128]{3,2,1,0:T(8,128)S(1)}, f32[6,44,8,128]{3,2,1,0:T(8,1...) custom-call(s32[1]{0:T(128)} %copy.39.lengths, ...), custom_call_target="tpu_custom_call" | custom-call | tf_op jit(solution)/shard_map/first_interior/pallas_call | solution.py:320
  6.7 0.0 collective-permute-done.on_got
  6.7 2.2 %collective-permute-done.1.cross_got = f32[76,8,128]{2,1,0:T(8,128)S(1)} collective-permute-done((f32[76,8,128]{2,1,0:T(8,128)S(1)}, f32[76,8,128]{2,1,0:T(8,128)S(1)}, u32[]{:S(2)}, u32[]{:S(2)}) %collective-permute-start.1) | collective-permute-done | bytes 311328 | tf_op jit(solution)/shard_map/ppermute | solution.py:311
  8.9 0.0 copy-start
  8.9 1.2 %first_boundary.1 = (f32[6,44,8,128]{3,2,1,0:T(8,128)S(1)}, f32[6,44,8,128]{3,2,1,0:T(8,128)S(1)}, f32[44,8,128]{2,1,0:T(8,128)S(1)}, f32[44,8,128]{2,1,0:T(8,12...) custom-call(s32[1]{0:T(128)} %copy.39.lengths, ...), custom_call_target="tpu_custom_call", output_to_operand_aliasing={{0}: (5, {}), {1}: (6, {}), {2}: (7, {}), {3}: (8, {}), {4}... | custom-call | tf_op jit(solution)/shard_map/first_boundary/pallas_call | solution.py:326
  10.1 1.7 %collective-permute-start.2 = (f32[36,8,128]{2,1,0:T(8,128)S(1)}, f32[36,8,128]{2,1,0:T(8,128)S(1)}, u32[]{:S(2)}, u32[]{:S(2)}) collective-permute-start(f32[36,8,128]{2,1,0:T(8,128)S(1)} %get-tuple-element.42), channel_id=1, source_target_pairs={{0,32},{32,0},{64,96},{96,64},{128,160},{160,128},{192,224},{224,1... | collective-permute-start | bytes 442376 | tf_op jit(solution)/shard_map/ppermute | solution.py:312
  11.8 0.0 collective-permute-start.3
  12.5 0.0 copy-done
  12.5 0.0 copy-start.2
  12.5 1.2 %second_interior.1 = (f32[6,44,8,128]{3,2,1,0:T(8,128)S(1)}, f32[6,44,8,128]{3,2,1,0:T(8,128)S(1)}, f32[6,44,8,128]{3,2,1,0:T(8,128)S(1)}, f32[32,128]{1,0:T(8,128)S(1)}, f32[32,128]{1,0:T(8,128)S(1)}) custom-call(s32[1]{0:T(128)} %copy.39.lengths, bf16[96,192]{1,0:T(8,128)(2,1)S(1)} %get-tuple-element.31.matrix, ...), custom_call_target="tpu_custom_call" | custom-call | tf_op jit(solution)/shard_map/second_interior/pallas_call | solution.py:333
  13.7 0.0 collective-permute-done.2.on_got
  13.7 2.7 %collective-permute-done.3.cross_got = f32[36,8,128]{2,1,0:T(8,128)S(1)} collective-permute-done((f32[36,8,128]{2,1,0:T(8,128)S(1)}, f32[36,8,128]{2,1,0:T(8,128)S(1)}, u32[]{:S(2)}, u32[]{:S(2)}) %collective-permute-start.3) | collective-permute-done | bytes 147488 | tf_op jit(solution)/shard_map/ppermute | solution.py:311
  16.4 0.0 copy-done.2
  16.4 1.2 %second_boundary.1 = (f32[6,44,8,128]{3,2,1,0:T(8,128)S(1)}, f32[6,44,8,128]{3,2,1,0:T(8,128)S(1)}, f32[6,44,8,128]{3,2,1,0:T(8,128)S(1)}, f32[6,44,8,128]{3,2,1,0:T(8,128)S(1)}, f32[32,128]{1,0:T(8,128)S(1)}) custom-call(s32[1]{0:T(128)} %copy.39.lengths, ...), custom_call_target="tpu_custom_call", output_to_operand_aliasing={{0}: (14, {}), {1}: (15, {}), {2}: (16, {}), {3}: (17, {})} | custom-call | tf_op jit(solution)/shard_map/second_boundary/pallas_call | solution.py:336
  17.6 2.0 %collective-permute-start.4 = (f32[32,128]{1,0:T(8,128)S(1)}, f32[32,128]{1,0:T(8,128)S(1)}, u32[]{:S(2)}, u32[]{:S(2)}) collective-permute-start(f32[32,128]{1,0:T(8,128)S(1)} %get-tuple-element.54), channel_id=1, source_target_pairs={{0,4},{1,5},{2,6},{3,7},{4,0},{5,1},{6,2},{7,3},{8,12},{9,13},{10,... | collective-permute-start | bytes 49160 | tf_op jit(solution)/shard_map/ppermute | solution.py:292
  19.6 3.3 %collective-permute-start.5 = (f32[32,128]{1,0:T(8,128)S(1)}, f32[32,128]{1,0:T(8,128)S(1)}, u32[]{:S(2)}, u32[]{:S(2)}) collective-permute-start(f32[32,128]{1,0:T(8,128)S(1)} %get-tuple-element.54), channel_id=1, source_target_pairs={{0,8},{1,9},{2,10},{3,11},{4,12},{5,13},{6,14},{7,15},{8,0},{9,1},... | collective-permute-start | bytes 49160 | tf_op jit(solution)/shard_map/ppermute | solution.py:292
  22.9 0.0 collective-permute-start.6
  22.9 1.0 %select_bitcast_fusion = f32[1,6,32,8,128]{4,3,2,1,0:T(8,128)} fusion(f32[6,44,8,128]{3,2,1,0:T(8,128)S(1)} %get-tuple-element.55, pred[32]{0:T(512)(128)(4,1)S(1)} %iota_compare_fusion), kind=kLoop, calls=%fused_computation | loop fusion | flops 196608 | bytes 1572896 | tf_op jit(solution)/shard_map/jit(_where)/select_n | solution.py:341
  23.9 0.0 collective-permute-done.4
  23.9 0.7 %collective-permute-done.5 = f32[32,128]{1,0:T(8,128)S(1)} collective-permute-done((f32[32,128]{1,0:T(8,128)S(1)}, f32[32,128]{1,0:T(8,128)S(1)}, u32[]{:S(2)}, u32[]{:S(2)}) %collective-permute-start.5) | collective-permute-done | bytes 16416 | tf_op jit(solution)/shard_map/ppermute | solution.py:292
  24.6 3.8 %collective-permute-done.6 = f32[32,128]{1,0:T(8,128)S(1)} collective-permute-done((f32[32,128]{1,0:T(8,128)S(1)}, f32[32,128]{1,0:T(8,128)S(1)}, u32[]{:S(2)}, u32[]{:S(2)}) %collective-permute-start.6) | collective-permute-done | bytes 16416 | tf_op jit(solution)/shard_map/ppermute | solution.py:292
  28.4 1.6 %collective-permute-start.7 = (f32[32,128]{1,0:T(8,128)S(1)}, f32[32,128]{1,0:T(8,128)S(1)}, u32[]{:S(2)}, u32[]{:S(2)}) collective-permute-start(f32[32,128]{1,0:T(8,128)S(1)} %add_add_fusion.1), channel_id=1, source_target_pairs={{0,1},{1,0},{2,3},{3,2},{4,5},{5,4},{6,7},{7,6},{8,9},{9,8},{10,11... | collective-permute-start | bytes 49160 | tf_op jit(solution)/shard_map/ppermute | solution.py:292
  30.0 2.9 %collective-permute-start.8 = (f32[32,128]{1,0:T(8,128)S(1)}, f32[32,128]{1,0:T(8,128)S(1)}, u32[]{:S(2)}, u32[]{:S(2)}) collective-permute-start(f32[32,128]{1,0:T(8,128)S(1)} %add_add_fusion.1), channel_id=1, source_target_pairs={{0,2},{1,3},{2,0},{3,1},{4,6},{5,7},{6,4},{7,5},{8,10},{9,11},{10,... | collective-permute-start | bytes 49160 | tf_op jit(solution)/shard_map/ppermute | solution.py:292
  32.9 0.2 collective-permute-start.9
  33.1 0.0 collective-permute-done.7
  33.1 2.1 %collective-permute-done.8 = f32[32,128]{1,0:T(8,128)S(1)} collective-permute-done((f32[32,128]{1,0:T(8,128)S(1)}, f32[32,128]{1,0:T(8,128)S(1)}, u32[]{:S(2)}, u32[]{:S(2)}) %collective-permute-start.8) | collective-permute-done | bytes 16416 | tf_op jit(solution)/shard_map/ppermute | solution.py:292
  35.2 2.6 %collective-permute-done.9 = f32[32,128]{1,0:T(8,128)S(1)} collective-permute-done((f32[32,128]{1,0:T(8,128)S(1)}, f32[32,128]{1,0:T(8,128)S(1)}, u32[]{:S(2)}, u32[]{:S(2)}) %collective-permute-start.9) | collective-permute-done | bytes 16416 | tf_op jit(solution)/shard_map/ppermute | solution.py:292
  37.9 3.1 %collective-permute-start.10 = (f32[32,128]{1,0:T(8,128)S(1)}, f32[32,128]{1,0:T(8,128)S(1)}, u32[]{:S(2)}, u32[]{:S(2)}) collective-permute-start(f32[32,128]{1,0:T(8,128)S(1)} %add_add_fusion), channel_id=1, source_target_pairs={{0,28},{1,29},{2,30},{3,31},{4,24},{5,25},{6,26},{7,27},{8,20},{9,... | collective-permute-start | bytes 49160 | tf_op jit(solution)/shard_map/ppermute | solution.py:292
  41.0 1.8 %collective-permute-done.10 = f32[32,128]{1,0:T(8,128)S(1)} collective-permute-done((f32[32,128]{1,0:T(8,128)S(1)}, f32[32,128]{1,0:T(8,128)S(1)}, u32[]{:S(2)}, u32[]{:S(2)}) %collective-permute-start.10) | collective-permute-done | bytes 16416 | tf_op jit(solution)/shard_map/ppermute | solution.py:292
  42.8 0.6 %add.27 = f32[32,128]{1,0:T(8,128)} add(f32[32,128]{1,0:T(8,128)S(1)} %add_add_fusion, f32[32,128]{1,0:T(8,128)S(1)} %collective-permute-done.10) | non-fusion elementwise | flops 4096 | bytes 49152 | tf_op jit(solution)/shard_map/add | solution.py:301
  (4 shorter events, 0.0 us)
Async XLA Ops:
  0.6 2.8 %copy-start.3 = (f32[1,2,6,6]{3,1,2,0:T(2,128)S(1)}, f32[1,2,6,6]{3,1,2,0:T(2,128)}, u32[]{:S(2)}) copy-start(f32[1,2,6,6]{3,1,2,0:T(2,128)} %param.16) | copy-start | bytes 868
  0.6 2.8 %copy-start.1 = (s32[1,2,128,128]{3,2,1,0:T(8,128)S(1)}, s32[1,2,128,128]{3,2,1,0:T(8,128)}, u32[]{:S(2)}) copy-start(s32[1,2,128,128]{3,2,1,0:T(8,128)} %perm.1) | copy-start | bytes 393220
  2.4 4.3 %collective-permute-start = (f32[76,8,128]{2,1,0:T(8,128)S(1)}, f32[76,8,128]{2,1,0:T(8,128)S(1)}, u32[]{:S(2)}, u32[]{:S(2)}) collective-permute-start(f32[76,8,128]{2,1,0:T(8,128)S(1)} %get-tuple-element.32), channel_id=1, source_target_pairs={{0,32},{32,0},{64,96},{96,64},{128,160},{160,128},{192,224},{224,1... | collective-permute-start | bytes 933896 | tf_op jit(solution)/shard_map/ppermute | solution.py:312
  2.5 6.4 %collective-permute-start.1 = (f32[76,8,128]{2,1,0:T(8,128)S(1)}, f32[76,8,128]{2,1,0:T(8,128)S(1)}, u32[]{:S(2)}, u32[]{:S(2)}) collective-permute-start(f32[76,8,128]{2,1,0:T(8,128)S(1)} %get-tuple-element.33), channel_id=1, source_target_pairs={{0,224},{32,64},{64,32},{96,128},{128,96},{160,192},{192,160},{224... | collective-permute-start | bytes 933896 | tf_op jit(solution)/shard_map/ppermute | solution.py:311
  8.9 3.6 %copy-start = (f32[1,6,32,128]{3,2,1,0:T(8,128)S(1)}, f32[1,6,32,128]{3,2,1,0:T(8,128)}, u32[]{:S(2)}) copy-start(f32[1,6,32,128]{3,2,1,0:T(8,128)} %wall_grad.3) | copy-start | bytes 294916
  10.1 3.6 %collective-permute-start.2 = (f32[36,8,128]{2,1,0:T(8,128)S(1)}, f32[36,8,128]{2,1,0:T(8,128)S(1)}, u32[]{:S(2)}, u32[]{:S(2)}) collective-permute-start(f32[36,8,128]{2,1,0:T(8,128)S(1)} %get-tuple-element.42), channel_id=1, source_target_pairs={{0,32},{32,0},{64,96},{96,64},{128,160},{160,128},{192,224},{224,1... | collective-permute-start | bytes 442376 | tf_op jit(solution)/shard_map/ppermute | solution.py:312
  11.8 4.6 %collective-permute-start.3 = (f32[36,8,128]{2,1,0:T(8,128)S(1)}, f32[36,8,128]{2,1,0:T(8,128)S(1)}, u32[]{:S(2)}, u32[]{:S(2)}) collective-permute-start(f32[36,8,128]{2,1,0:T(8,128)S(1)} %get-tuple-element.43), channel_id=1, source_target_pairs={{0,224},{32,64},{64,32},{96,128},{128,96},{160,192},{192,160},{224... | collective-permute-start | bytes 442376 | tf_op jit(solution)/shard_map/ppermute | solution.py:311
  12.5 3.9 %copy-start.2 = (s32[32,128]{1,0:T(8,128)S(1)}, s32[32,128]{1,0:T(8,128)}, u32[]{:S(2)}) copy-start(s32[32,128]{1,0:T(8,128)} %wall_mask.1) | copy-start | bytes 49156
  17.6 6.3 %collective-permute-start.4 = (f32[32,128]{1,0:T(8,128)S(1)}, f32[32,128]{1,0:T(8,128)S(1)}, u32[]{:S(2)}, u32[]{:S(2)}) collective-permute-start(f32[32,128]{1,0:T(8,128)S(1)} %get-tuple-element.54), channel_id=1, source_target_pairs={{0,4},{1,5},{2,6},{3,7},{4,0},{5,1},{6,2},{7,3},{8,12},{9,13},{10,... | collective-permute-start | bytes 49160 | tf_op jit(solution)/shard_map/ppermute | solution.py:292
  19.6 5.0 %collective-permute-start.5 = (f32[32,128]{1,0:T(8,128)S(1)}, f32[32,128]{1,0:T(8,128)S(1)}, u32[]{:S(2)}, u32[]{:S(2)}) collective-permute-start(f32[32,128]{1,0:T(8,128)S(1)} %get-tuple-element.54), channel_id=1, source_target_pairs={{0,8},{1,9},{2,10},{3,11},{4,12},{5,13},{6,14},{7,15},{8,0},{9,1},... | collective-permute-start | bytes 49160 | tf_op jit(solution)/shard_map/ppermute | solution.py:292
  22.9 5.5 %collective-permute-start.6 = (f32[32,128]{1,0:T(8,128)S(1)}, f32[32,128]{1,0:T(8,128)S(1)}, u32[]{:S(2)}, u32[]{:S(2)}) collective-permute-start(f32[32,128]{1,0:T(8,128)S(1)} %get-tuple-element.54), channel_id=1, source_target_pairs={{0,12},{1,13},{2,14},{3,15},{4,8},{5,9},{6,10},{7,11},{8,4},{9,5},... | collective-permute-start | bytes 49160 | tf_op jit(solution)/shard_map/ppermute | solution.py:292
  28.4 4.7 %collective-permute-start.7 = (f32[32,128]{1,0:T(8,128)S(1)}, f32[32,128]{1,0:T(8,128)S(1)}, u32[]{:S(2)}, u32[]{:S(2)}) collective-permute-start(f32[32,128]{1,0:T(8,128)S(1)} %add_add_fusion.1), channel_id=1, source_target_pairs={{0,1},{1,0},{2,3},{3,2},{4,5},{5,4},{6,7},{7,6},{8,9},{9,8},{10,11... | collective-permute-start | bytes 49160 | tf_op jit(solution)/shard_map/ppermute | solution.py:292
  30.0 5.2 %collective-permute-start.8 = (f32[32,128]{1,0:T(8,128)S(1)}, f32[32,128]{1,0:T(8,128)S(1)}, u32[]{:S(2)}, u32[]{:S(2)}) collective-permute-start(f32[32,128]{1,0:T(8,128)S(1)} %add_add_fusion.1), channel_id=1, source_target_pairs={{0,2},{1,3},{2,0},{3,1},{4,6},{5,7},{6,4},{7,5},{8,10},{9,11},{10,... | collective-permute-start | bytes 49160 | tf_op jit(solution)/shard_map/ppermute | solution.py:292
  32.9 4.9 %collective-permute-start.9 = (f32[32,128]{1,0:T(8,128)S(1)}, f32[32,128]{1,0:T(8,128)S(1)}, u32[]{:S(2)}, u32[]{:S(2)}) collective-permute-start(f32[32,128]{1,0:T(8,128)S(1)} %add_add_fusion.1), channel_id=1, source_target_pairs={{0,3},{1,2},{2,1},{3,0},{4,7},{5,6},{6,5},{7,4},{8,11},{9,10},{10,... | collective-permute-start | bytes 49160 | tf_op jit(solution)/shard_map/ppermute | solution.py:292
  37.9 4.9 %collective-permute-start.10 = (f32[32,128]{1,0:T(8,128)S(1)}, f32[32,128]{1,0:T(8,128)S(1)}, u32[]{:S(2)}, u32[]{:S(2)}) collective-permute-start(f32[32,128]{1,0:T(8,128)S(1)} %add_add_fusion), channel_id=1, source_target_pairs={{0,28},{1,29},{2,30},{3,31},{4,24},{5,25},{6,26},{7,27},{8,20},{9,... | collective-permute-start | bytes 49160 | tf_op jit(solution)/shard_map/ppermute | solution.py:292

commit v2 on v1

--- a/solution.py
+++ b/solution.py
@@ -37,7 +37,7 @@
             at += depth
 
 
-def pack_kernel(lengths, state, source, second, fourth, step, on_send, cross_send, sem):
+def pack_kernel(lengths, state, source, second, fourth, step, cross_send, on_send, sem):
     refs = {"state": state, "source": source, "second": second, "fourth": fourth, "step": step}
     odd = odd_place()
 
@@ -208,8 +208,8 @@
 
 
 def first_boundary_kernel(
-    lengths, index, matrix, on_got, cross_got, state_in, source_in, second_in, fourth_in, step_in, one_in, two_in, three_in,
-    state, source, second, fourth, step, one, two, three, on_send, cross_send,
+    lengths, index, matrix, cross_got, on_got, state_in, source_in, second_in, fourth_in, step_in, one_in, two_in, three_in,
+    state, source, second, fourth, step, one, two, three, cross_send, on_send,
 ):
     active_len = lengths[0]
     refs = {"state": state, "source": source, "second": second, "fourth": fourth, "step": step}
@@ -246,7 +246,7 @@
 
 
 def second_boundary_kernel(
-    lengths, weight, index, matrix, on_got, cross_got, source, second, fourth, step, wall_grad, wall_mask, wall_start, wall_in,
+    lengths, weight, index, matrix, cross_got, on_got, source, second, fourth, step, wall_grad, wall_mask, wall_start, wall_in,
     state_in, one_in, two_in, three_in,
     state, one, two, three, wall,
     rows,
@@ -295,9 +295,9 @@
         copies = jnp.broadcast_to(value[None], (len(groups[0]),) + value.shape)
         return lax.all_to_all(copies, "cond", 0, 0, tiled=True, axis_index_groups=groups).sum(0)
 
-    value = value + move(value, lambda z: z ^ 1, same) + move(value, lambda z: z ^ 2, same) + move(value, lambda z: z ^ 3, same)
+    value = value + move(value, lambda z: z ^ 3, same) + move(value, lambda z: z ^ 2, same) + move(value, lambda z: z ^ 1, same)
     value, adjoint = lax.optimization_barrier((value, adjoint))
-    value = value + move(value, same, lambda y: y ^ 1) + move(value, same, lambda y: y ^ 2) + move(value, same, lambda y: y ^ 3)
+    value = value + move(value, same, lambda y: y ^ 2) + move(value, same, lambda y: y ^ 3) + move(value, same, lambda y: y ^ 1)
     value = value + move(value, lambda z: 7 - z, same)
     return adjoint, value
 
@@ -313,7 +313,7 @@
 
     planes, plane = f32(NV, EXT, J, K), f32(EXT, J, K)
     inputs = [pltpu.with_memory_space_constraint(x, pltpu.HBM) for x in (adjoint_in, source, second_coef, fourth_coef, time_step)]
-    on_send, cross_send = call(
+    cross_send, on_send = call(
         pack_kernel, "pack_rims", [f32(PLANES, J, K)] * 2, [SMEM] + [HBM] * 5, scratch=[pltpu.SemaphoreType.DMA((2,))],
     )(lengths, *inputs)
     on_got, cross_got = exchange(on_send, cross_send)
@@ -323,11 +323,11 @@
          plane, plane, plane, planes, planes, planes],
         [SMEM, SMEM, VMEM] + [HBM] * 5, scratch=[pltpu.SemaphoreType.DMA((5,))],
     )(lengths, jacobians, face_perm, *inputs)
-    _, source_x, second_x, fourth_x, step_x, _, _, three, on_send, cross_send = call(
+    _, source_x, second_x, fourth_x, step_x, _, _, three, cross_send, on_send = call(
         first_boundary_kernel, "first_boundary",
         [planes, planes, plane, plane, plane, planes, planes, planes] + [f32(NV * DEEP, J, K)] * 2,
         [SMEM] + [VMEM] * 12, aliases={5 + n: n for n in range(8)},
-    )(lengths, index, matrix, on_got, cross_got, *arrays)
+    )(lengths, index, matrix, cross_got, on_got, *arrays)
     fields = (source_x, second_x, fourth_x, step_x)
     on_got, cross_got = exchange(on_send, cross_send)
     four, five, six, wall_start, wall = call(
@@ -336,7 +336,7 @@
     _, _, _, six, wall = call(
         second_boundary_kernel, "second_boundary", [planes] * 4 + [f32(SLOTS, K)],
         [SMEM] * 2 + [VMEM] * 16, scratch=[pltpu.VMEM((SLOTS, K), jnp.float32)], aliases={14 + n: n for n in range(4)},
-    )(lengths, cond_weight, index, matrix, on_got, cross_got, *fields, wall_grad, wall_mask, wall_start, wall, three, four, five, six)
+    )(lengths, cond_weight, index, matrix, cross_got, on_got, *fields, wall_grad, wall_mask, wall_start, wall, three, four, five, six)
     active = lax.iota(jnp.int32, SLOTS) < lengths[0]
     adjoint = jnp.where(active[None, None, :, None, None], six[None, :, DEEP : DEEP + SLOTS], 0.0)
     return sum_over_conditions(wall, adjoint, z_size, y_size)

time: 43.6 us -> 42.3 us (0.970)
  the two profiles are of different devices: /device:TPU:6 before, /device:TPU:32 now
where the time goes in v2:
time: 42.3 us; the launch traced here: 42 us
  starting transfers between devices  18.8 us (44%)
  waiting for transfers between devices  11.1 us (26%)
  Pallas kernels  8.44 us (20%)
  between operations  2.06 us (5%)
  other arithmetic  1.63 us (4%)
    ppermute x7, starting transfers between devices, move(): return lax.ppermute(value, 'cond', pairs(z_to, y_to))  14.2 us
    ppermute x7, waiting for transfers between devices, move(): return lax.ppermute(value, 'cond', pairs(z_to, y_to))  7.75 us
    ppermute x2, starting transfers between devices, exchange(): cross_got = lax.ppermute(cross_send, 'blk', cross)  4.52 us
    pallas_call x1, Pallas kernels, body(): call(first_interior_kernel, 'first_interior', [jax.ShapeDtypeStruct((2, J...  3.52 us
    ppermute x2, waiting for transfers between devices, exchange(): cross_got = lax.ppermute(cross_send, 'blk', cross)  3.31 us
    pallas_call x1, Pallas kernels, body(): call(second_interior_kernel, 'second_interior', [planes] * 3 + [f32(SLOTS...  1.41 us
    pallas_call x1, Pallas kernels, body(): call(second_boundary_kernel, 'second_boundary', [planes] * 4 + [f32(SLOTS...  1.24 us
    pallas_call x1, Pallas kernels, body(): call(first_boundary_kernel, 'first_boundary', [planes, planes, plane, pla...  1.21 us
  transfers between devices with their start and end apart: 11, of which 7 were waited for; matrix products, arithmetic and copies ran while one was open for 2% of the time, Pallas kernels for 12%

profile of v2, /device:TPU:32, one launch (start us, length us, event | category | flops | bytes accessed | tf_op | source)
XLA Modules:
  0.0 42.0 jit_solution(7519374033524633387)
XLA Ops:
  0.6 0.0 copy-start.3
  0.6 0.0 copy-start.1
  1.3 1.1 %pack_rims.1 = (f32[76,8,128]{2,1,0:T(8,128)S(1)}, f32[76,8,128]{2,1,0:T(8,128)S(1)}) custom-call(s32[1]{0:T(128)} %copy.39.lengths, f32[1,6,32,8,128]{4,3,2,1,0:T(8,128)} %state.1, f32[1,6,32,8,128]{4,3,2,1,0:T(8,128)} %source.1, f32[1,32,8,128]{3,2,1,0:T(8,128)} %second.1, f32[1,32,8,128]{3,2,1,0:T(8,128)} %fourth.1, f32[1,32,8,128]{3,2,1,0:T(8,128)} %step.1), custom_call_target="tpu_custom_call" | custom-call | tf_op jit(solution)/shard_map/pack_rims/pallas_call | solution.py:316
  2.4 2.3 %collective-permute-start = (f32[76,8,128]{2,1,0:T(8,128)S(1)}, f32[76,8,128]{2,1,0:T(8,128)S(1)}, u32[]{:S(2)}, u32[]{:S(2)}) collective-permute-start(f32[76,8,128]{2,1,0:T(8,128)S(1)} %get-tuple-element.32), channel_id=1, source_target_pairs={{0,224},{32,64},{64,32},{96,128},{128,96},{160,192},{192,160},{224... | collective-permute-start | bytes 933896 | tf_op jit(solution)/shard_map/ppermute | solution.py:311
  4.7 0.0 collective-permute-start.1
  4.7 0.0 copy-done.3
  4.7 0.0 copy-done.1
  4.7 3.5 %first_interior.1 = (s32[2,8,128]{2,1,0:T(8,128)S(1)}, bf16[96,192]{1,0:T(8,128)(2,1)S(1)}, f32[6,44,8,128]{3,2,1,0:T(8,128)S(1)}, f32[6,44,8,128]{3,2,1,0:T(8,1...) custom-call(s32[1]{0:T(128)} %copy.39.lengths, ...), custom_call_target="tpu_custom_call" | custom-call | tf_op jit(solution)/shard_map/first_interior/pallas_call | solution.py:320
  8.2 1.8 %collective-permute-done.cross_got = f32[76,8,128]{2,1,0:T(8,128)S(1)} collective-permute-done((f32[76,8,128]{2,1,0:T(8,128)S(1)}, f32[76,8,128]{2,1,0:T(8,128)S(1)}, u32[]{:S(2)}, u32[]{:S(2)}) %collective-permute-start) | collective-permute-done | bytes 311328 | tf_op jit(solution)/shard_map/ppermute | solution.py:311
  10.0 0.0 collective-permute-done.1.on_got
  10.0 0.0 copy-start
  10.0 1.2 %first_boundary.1 = (f32[6,44,8,128]{3,2,1,0:T(8,128)S(1)}, f32[6,44,8,128]{3,2,1,0:T(8,128)S(1)}, f32[44,8,128]{2,1,0:T(8,128)S(1)}, f32[44,8,128]{2,1,0:T(8,12...) custom-call(s32[1]{0:T(128)} %copy.39.lengths, ...), custom_call_target="tpu_custom_call", output_to_operand_aliasing={{0}: (5, {}), {1}: (6, {}), {2}: (7, {}), {3}: (8, {}), {4}... | custom-call | tf_op jit(solution)/shard_map/first_boundary/pallas_call | solution.py:326
  11.2 2.3 %collective-permute-start.2 = (f32[36,8,128]{2,1,0:T(8,128)S(1)}, f32[36,8,128]{2,1,0:T(8,128)S(1)}, u32[]{:S(2)}, u32[]{:S(2)}) collective-permute-start(f32[36,8,128]{2,1,0:T(8,128)S(1)} %get-tuple-element.42), channel_id=1, source_target_pairs={{0,224},{32,64},{64,32},{96,128},{128,96},{160,192},{192,160},{224... | collective-permute-start | bytes 442376 | tf_op jit(solution)/shard_map/ppermute | solution.py:311
  13.5 0.0 collective-permute-start.3
  14.2 0.0 copy-done
  14.2 0.0 copy-start.2
  14.2 1.4 %second_interior.1 = (f32[6,44,8,128]{3,2,1,0:T(8,128)S(1)}, f32[6,44,8,128]{3,2,1,0:T(8,128)S(1)}, f32[6,44,8,128]{3,2,1,0:T(8,128)S(1)}, f32[32,128]{1,0:T(8,128)S(1)}, f32[32,128]{1,0:T(8,128)S(1)}) custom-call(s32[1]{0:T(128)} %copy.39.lengths, bf16[96,192]{1,0:T(8,128)(2,1)S(1)} %get-tuple-element.31.matrix, ...), custom_call_target="tpu_custom_call" | custom-call | tf_op jit(solution)/shard_map/second_interior/pallas_call | solution.py:333
  15.6 1.5 %collective-permute-done.2.cross_got = f32[36,8,128]{2,1,0:T(8,128)S(1)} collective-permute-done((f32[36,8,128]{2,1,0:T(8,128)S(1)}, f32[36,8,128]{2,1,0:T(8,128)S(1)}, u32[]{:S(2)}, u32[]{:S(2)}) %collective-permute-start.2) | collective-permute-done | bytes 147488 | tf_op jit(solution)/shard_map/ppermute | solution.py:311
  17.1 0.0 collective-permute-done.3.on_got
  17.1 0.0 copy-done.2
  17.1 1.2 %second_boundary.1 = (f32[6,44,8,128]{3,2,1,0:T(8,128)S(1)}, f32[6,44,8,128]{3,2,1,0:T(8,128)S(1)}, f32[6,44,8,128]{3,2,1,0:T(8,128)S(1)}, f32[6,44,8,128]{3,2,1,0:T(8,128)S(1)}, f32[32,128]{1,0:T(8,128)S(1)}) custom-call(s32[1]{0:T(128)} %copy.39.lengths, ...), custom_call_target="tpu_custom_call", output_to_operand_aliasing={{0}: (14, {}), {1}: (15, {}), {2}: (16, {}), {3}: (17, {})} | custom-call | tf_op jit(solution)/shard_map/second_boundary/pallas_call | solution.py:336
  18.4 2.0 %collective-permute-start.4 = (f32[32,128]{1,0:T(8,128)S(1)}, f32[32,128]{1,0:T(8,128)S(1)}, u32[]{:S(2)}, u32[]{:S(2)}) collective-permute-start(f32[32,128]{1,0:T(8,128)S(1)} %get-tuple-element.54), channel_id=1, source_target_pairs={{0,12},{1,13},{2,14},{3,15},{4,8},{5,9},{6,10},{7,11},{8,4},{9,5},... | collective-permute-start | bytes 49160 | tf_op jit(solution)/shard_map/ppermute | solution.py:292
  20.4 2.3 %collective-permute-start.5 = (f32[32,128]{1,0:T(8,128)S(1)}, f32[32,128]{1,0:T(8,128)S(1)}, u32[]{:S(2)}, u32[]{:S(2)}) collective-permute-start(f32[32,128]{1,0:T(8,128)S(1)} %get-tuple-element.54), channel_id=1, source_target_pairs={{0,8},{1,9},{2,10},{3,11},{4,12},{5,13},{6,14},{7,15},{8,0},{9,1},... | collective-permute-start | bytes 49160 | tf_op jit(solution)/shard_map/ppermute | solution.py:292
  22.6 0.5 %collective-permute-start.6 = (f32[32,128]{1,0:T(8,128)S(1)}, f32[32,128]{1,0:T(8,128)S(1)}, u32[]{:S(2)}, u32[]{:S(2)}) collective-permute-start(f32[32,128]{1,0:T(8,128)S(1)} %get-tuple-element.54), channel_id=1, source_target_pairs={{0,4},{1,5},{2,6},{3,7},{4,0},{5,1},{6,2},{7,3},{8,12},{9,13},{10,... | collective-permute-start | bytes 49160 | tf_op jit(solution)/shard_map/ppermute | solution.py:292
  23.2 1.0 %select_bitcast_fusion = f32[1,6,32,8,128]{4,3,2,1,0:T(8,128)} fusion(f32[6,44,8,128]{3,2,1,0:T(8,128)S(1)} %get-tuple-element.55, pred[32]{0:T(512)(128)(4,1)S(1)} %iota_compare_fusion), kind=kLoop, calls=%fused_computation | loop fusion | flops 196608 | bytes 1572896 | tf_op jit(solution)/shard_map/jit(_where)/select_n | solution.py:341
  24.2 0.0 collective-permute-done.4
  24.2 0.8 %collective-permute-done.5 = f32[32,128]{1,0:T(8,128)S(1)} collective-permute-done((f32[32,128]{1,0:T(8,128)S(1)}, f32[32,128]{1,0:T(8,128)S(1)}, u32[]{:S(2)}, u32[]{:S(2)}) %collective-permute-start.5) | collective-permute-done | bytes 16416 | tf_op jit(solution)/shard_map/ppermute | solution.py:292
  25.0 1.4 %collective-permute-done.6 = f32[32,128]{1,0:T(8,128)S(1)} collective-permute-done((f32[32,128]{1,0:T(8,128)S(1)}, f32[32,128]{1,0:T(8,128)S(1)}, u32[]{:S(2)}, u32[]{:S(2)}) %collective-permute-start.6) | collective-permute-done | bytes 16416 | tf_op jit(solution)/shard_map/ppermute | solution.py:292
  26.4 2.4 %collective-permute-start.7 = (f32[32,128]{1,0:T(8,128)S(1)}, f32[32,128]{1,0:T(8,128)S(1)}, u32[]{:S(2)}, u32[]{:S(2)}) collective-permute-start(f32[32,128]{1,0:T(8,128)S(1)} %add_add_fusion.1), channel_id=1, source_target_pairs={{0,2},{1,3},{2,0},{3,1},{4,6},{5,7},{6,4},{7,5},{8,10},{9,11},{10,... | collective-permute-start | bytes 49160 | tf_op jit(solution)/shard_map/ppermute | solution.py:292
  28.7 1.0 %collective-permute-start.8 = (f32[32,128]{1,0:T(8,128)S(1)}, f32[32,128]{1,0:T(8,128)S(1)}, u32[]{:S(2)}, u32[]{:S(2)}) collective-permute-start(f32[32,128]{1,0:T(8,128)S(1)} %add_add_fusion.1), channel_id=1, source_target_pairs={{0,3},{1,2},{2,1},{3,0},{4,7},{5,6},{6,5},{7,4},{8,11},{9,10},{10,... | collective-permute-start | bytes 49160 | tf_op jit(solution)/shard_map/ppermute | solution.py:292
  29.8 0.1 collective-permute-start.9
  29.9 1.8 %collective-permute-done.7 = f32[32,128]{1,0:T(8,128)S(1)} collective-permute-done((f32[32,128]{1,0:T(8,128)S(1)}, f32[32,128]{1,0:T(8,128)S(1)}, u32[]{:S(2)}, u32[]{:S(2)}) %collective-permute-start.7) | collective-permute-done | bytes 16416 | tf_op jit(solution)/shard_map/ppermute | solution.py:292
  31.6 2.1 %collective-permute-done.8 = f32[32,128]{1,0:T(8,128)S(1)} collective-permute-done((f32[32,128]{1,0:T(8,128)S(1)}, f32[32,128]{1,0:T(8,128)S(1)}, u32[]{:S(2)}, u32[]{:S(2)}) %collective-permute-start.8) | collective-permute-done | bytes 16416 | tf_op jit(solution)/shard_map/ppermute | solution.py:292
  33.7 0.0 collective-permute-done.9
  33.7 5.9 %collective-permute-start.10 = (f32[32,128]{1,0:T(8,128)S(1)}, f32[32,128]{1,0:T(8,128)S(1)}, u32[]{:S(2)}, u32[]{:S(2)}) collective-permute-start(f32[32,128]{1,0:T(8,128)S(1)} %add_add_fusion), channel_id=1, source_target_pairs={{0,28},{1,29},{2,30},{3,31},{4,24},{5,25},{6,26},{7,27},{8,20},{9,... | collective-permute-start | bytes 49160 | tf_op jit(solution)/shard_map/ppermute | solution.py:292
  39.6 1.7 %collective-permute-done.10 = f32[32,128]{1,0:T(8,128)S(1)} collective-permute-done((f32[32,128]{1,0:T(8,128)S(1)}, f32[32,128]{1,0:T(8,128)S(1)}, u32[]{:S(2)}, u32[]{:S(2)}) %collective-permute-start.10) | collective-permute-done | bytes 16416 | tf_op jit(solution)/shard_map/ppermute | solution.py:292
  41.4 0.6 %add.27 = f32[32,128]{1,0:T(8,128)} add(f32[32,128]{1,0:T(8,128)S(1)} %add_add_fusion, f32[32,128]{1,0:T(8,128)S(1)} %collective-permute-done.10) | non-fusion elementwise | flops 4096 | bytes 49152 | tf_op jit(solution)/shard_map/add | solution.py:301
  (4 shorter events, 0.0 us)
Async XLA Ops:
  0.6 4.0 %copy-start.3 = (f32[1,2,6,6]{3,1,2,0:T(2,128)S(1)}, f32[1,2,6,6]{3,1,2,0:T(2,128)}, u32[]{:S(2)}) copy-start(f32[1,2,6,6]{3,1,2,0:T(2,128)} %param.16) | copy-start | bytes 868
  0.6 4.0 %copy-start.1 = (s32[1,2,128,128]{3,2,1,0:T(8,128)S(1)}, s32[1,2,128,128]{3,2,1,0:T(8,128)}, u32[]{:S(2)}) copy-start(s32[1,2,128,128]{3,2,1,0:T(8,128)} %perm.1) | copy-start | bytes 393220
  2.4 7.6 %collective-permute-start = (f32[76,8,128]{2,1,0:T(8,128)S(1)}, f32[76,8,128]{2,1,0:T(8,128)S(1)}, u32[]{:S(2)}, u32[]{:S(2)}) collective-permute-start(f32[76,8,128]{2,1,0:T(8,128)S(1)} %get-tuple-element.32), channel_id=1, source_target_pairs={{0,224},{32,64},{64,32},{96,128},{128,96},{160,192},{192,160},{224... | collective-permute-start | bytes 933896 | tf_op jit(solution)/shard_map/ppermute | solution.py:311
  4.7 5.4 %collective-permute-start.1 = (f32[76,8,128]{2,1,0:T(8,128)S(1)}, f32[76,8,128]{2,1,0:T(8,128)S(1)}, u32[]{:S(2)}, u32[]{:S(2)}) collective-permute-start(f32[76,8,128]{2,1,0:T(8,128)S(1)} %get-tuple-element.33), channel_id=1, source_target_pairs={{0,32},{32,0},{64,96},{96,64},{128,160},{160,128},{192,224},{224,1... | collective-permute-start | bytes 933896 | tf_op jit(solution)/shard_map/ppermute | solution.py:312
  10.0 4.1 %copy-start = (f32[1,6,32,128]{3,2,1,0:T(8,128)S(1)}, f32[1,6,32,128]{3,2,1,0:T(8,128)}, u32[]{:S(2)}) copy-start(f32[1,6,32,128]{3,2,1,0:T(8,128)} %wall_grad.3) | copy-start | bytes 294916
  11.2 5.9 %collective-permute-start.2 = (f32[36,8,128]{2,1,0:T(8,128)S(1)}, f32[36,8,128]{2,1,0:T(8,128)S(1)}, u32[]{:S(2)}, u32[]{:S(2)}) collective-permute-start(f32[36,8,128]{2,1,0:T(8,128)S(1)} %get-tuple-element.42), channel_id=1, source_target_pairs={{0,224},{32,64},{64,32},{96,128},{128,96},{160,192},{192,160},{224... | collective-permute-start | bytes 442376 | tf_op jit(solution)/shard_map/ppermute | solution.py:311
  13.5 3.6 %collective-permute-start.3 = (f32[36,8,128]{2,1,0:T(8,128)S(1)}, f32[36,8,128]{2,1,0:T(8,128)S(1)}, u32[]{:S(2)}, u32[]{:S(2)}) collective-permute-start(f32[36,8,128]{2,1,0:T(8,128)S(1)} %get-tuple-element.43), channel_id=1, source_target_pairs={{0,32},{32,0},{64,96},{96,64},{128,160},{160,128},{192,224},{224,1... | collective-permute-start | bytes 442376 | tf_op jit(solution)/shard_map/ppermute | solution.py:312
  14.2 2.9 %copy-start.2 = (s32[32,128]{1,0:T(8,128)S(1)}, s32[32,128]{1,0:T(8,128)}, u32[]{:S(2)}) copy-start(s32[32,128]{1,0:T(8,128)} %wall_mask.1) | copy-start | bytes 49156
  18.4 5.8 %collective-permute-start.4 = (f32[32,128]{1,0:T(8,128)S(1)}, f32[32,128]{1,0:T(8,128)S(1)}, u32[]{:S(2)}, u32[]{:S(2)}) collective-permute-start(f32[32,128]{1,0:T(8,128)S(1)} %get-tuple-element.54), channel_id=1, source_target_pairs={{0,12},{1,13},{2,14},{3,15},{4,8},{5,9},{6,10},{7,11},{8,4},{9,5},... | collective-permute-start | bytes 49160 | tf_op jit(solution)/shard_map/ppermute | solution.py:292
  20.4 4.6 %collective-permute-start.5 = (f32[32,128]{1,0:T(8,128)S(1)}, f32[32,128]{1,0:T(8,128)S(1)}, u32[]{:S(2)}, u32[]{:S(2)}) collective-permute-start(f32[32,128]{1,0:T(8,128)S(1)} %get-tuple-element.54), channel_id=1, source_target_pairs={{0,8},{1,9},{2,10},{3,11},{4,12},{5,13},{6,14},{7,15},{8,0},{9,1},... | collective-permute-start | bytes 49160 | tf_op jit(solution)/shard_map/ppermute | solution.py:292
  22.6 3.7 %collective-permute-start.6 = (f32[32,128]{1,0:T(8,128)S(1)}, f32[32,128]{1,0:T(8,128)S(1)}, u32[]{:S(2)}, u32[]{:S(2)}) collective-permute-start(f32[32,128]{1,0:T(8,128)S(1)} %get-tuple-element.54), channel_id=1, source_target_pairs={{0,4},{1,5},{2,6},{3,7},{4,0},{5,1},{6,2},{7,3},{8,12},{9,13},{10,... | collective-permute-start | bytes 49160 | tf_op jit(solution)/shard_map/ppermute | solution.py:292
  26.4 5.2 %collective-permute-start.7 = (f32[32,128]{1,0:T(8,128)S(1)}, f32[32,128]{1,0:T(8,128)S(1)}, u32[]{:S(2)}, u32[]{:S(2)}) collective-permute-start(f32[32,128]{1,0:T(8,128)S(1)} %add_add_fusion.1), channel_id=1, source_target_pairs={{0,2},{1,3},{2,0},{3,1},{4,6},{5,7},{6,4},{7,5},{8,10},{9,11},{10,... | collective-permute-start | bytes 49160 | tf_op jit(solution)/shard_map/ppermute | solution.py:292
  28.7 4.9 %collective-permute-start.8 = (f32[32,128]{1,0:T(8,128)S(1)}, f32[32,128]{1,0:T(8,128)S(1)}, u32[]{:S(2)}, u32[]{:S(2)}) collective-permute-start(f32[32,128]{1,0:T(8,128)S(1)} %add_add_fusion.1), channel_id=1, source_target_pairs={{0,3},{1,2},{2,1},{3,0},{4,7},{5,6},{6,5},{7,4},{8,11},{9,10},{10,... | collective-permute-start | bytes 49160 | tf_op jit(solution)/shard_map/ppermute | solution.py:292
  29.8 3.9 %collective-permute-start.9 = (f32[32,128]{1,0:T(8,128)S(1)}, f32[32,128]{1,0:T(8,128)S(1)}, u32[]{:S(2)}, u32[]{:S(2)}) collective-permute-start(f32[32,128]{1,0:T(8,128)S(1)} %add_add_fusion.1), channel_id=1, source_target_pairs={{0,1},{1,0},{2,3},{3,2},{4,5},{5,4},{6,7},{7,6},{8,9},{9,8},{10,11... | collective-permute-start | bytes 49160 | tf_op jit(solution)/shard_map/ppermute | solution.py:292
  33.7 7.7 %collective-permute-start.10 = (f32[32,128]{1,0:T(8,128)S(1)}, f32[32,128]{1,0:T(8,128)S(1)}, u32[]{:S(2)}, u32[]{:S(2)}) collective-permute-start(f32[32,128]{1,0:T(8,128)S(1)} %add_add_fusion), channel_id=1, source_target_pairs={{0,28},{1,29},{2,30},{3,31},{4,24},{5,25},{6,26},{7,27},{8,20},{9,... | collective-permute-start | bytes 49160 | tf_op jit(solution)/shard_map/ppermute | solution.py:292

commit v3 on v2

--- a/solution.py
+++ b/solution.py
@@ -16,7 +16,7 @@
 EXT = SLOTS + 2 * DEEP
 PLANES = NV * DEEP + 2 * DEEP + NV * NEAR + NEAR
 FACTORS = (0.6, 0.6, 1.0)
-GROUP = 8
+GROUPS = (14, 12, 10)
 ROWS = NV * J
 
 VMEM = pl.BlockSpec(memory_space=pltpu.VMEM)
@@ -150,11 +150,12 @@
     anchor = states[0]
     for s in range(3):
         lead = 2 * (s + 1)
-        groups = lax.div(jnp.maximum(active_len - 2 * lead, 0) + (GROUP - 1), GROUP)
-
-        def step(g, _, s=s, lead=lead):
-            first = DEEP + lead + g * GROUP
-            advance(FACTORS[s], matrix[...], [(first, GROUP)], anchor, states[s], states[s + 1], fields)
+        size = GROUPS[s]
+        groups = lax.div(jnp.maximum(active_len - 2 * lead, 0) + (size - 1), size)
+
+        def step(g, _, s=s, lead=lead, size=size):
+            first = DEEP + lead + g * size
+            advance(FACTORS[s], matrix[...], [(first, size)], anchor, states[s], states[s + 1], fields)
             return 0
 
         lax.fori_loop(0, groups, step, 0)
@@ -295,9 +296,9 @@
         copies = jnp.broadcast_to(value[None], (len(groups[0]),) + value.shape)
         return lax.all_to_all(copies, "cond", 0, 0, tiled=True, axis_index_groups=groups).sum(0)
 
-    value = value + move(value, lambda z: z ^ 3, same) + move(value, lambda z: z ^ 2, same) + move(value, lambda z: z ^ 1, same)
+    value = value + move(value, lambda z: z ^ 2, same) + move(value, lambda z: z ^ 3, same) + move(value, lambda z: z ^ 1, same)
     value, adjoint = lax.optimization_barrier((value, adjoint))
-    value = value + move(value, same, lambda y: y ^ 2) + move(value, same, lambda y: y ^ 3) + move(value, same, lambda y: y ^ 1)
+    value = value + move(value, same, lambda y: y ^ 2) + move(value, same, lambda y: y ^ 1) + move(value, same, lambda y: y ^ 3)
     value = value + move(value, lambda z: 7 - z, same)
     return adjoint, value
 

time: 42.3 us -> 41.9 us (level)
  Pallas kernels: 8.44 us -> 7.36 us
  waiting for transfers between devices: 11.1 us -> 11.8 us
    ppermute x2, waiting for transfers between devices: 3.31 us -> 4.31 us  [exchange(): cross_got = lax.ppermute(cross_send, 'blk', cross)]
    pallas_call x1, Pallas kernels: 3.52 us -> 2.97 us  [body(): call(first_interior_kernel, 'first_interior', [jax.ShapeDtypeStruct((2, J...]
    pallas_call x1, Pallas kernels: 1.41 us -> 0.88 us  [body(): call(second_interior_kernel, 'second_interior', [planes] * 3 + [f32(SLOTS...]
  transfers between devices with their start and end apart: 11 -> 11, of which waited for: 7 -> 7; matrix products, arithmetic and copies ran while one was open for 2% -> 2% of each run, Pallas kernels for 12% -> 9%
where the time goes in v3:
time: 41.9 us; the launch traced here: 41.7 us
  starting transfers between devices  18.9 us (45%)
  waiting for transfers between devices  11.8 us (28%)
  Pallas kernels  7.36 us (18%)
  between operations  2.05 us (5%)
  other arithmetic  1.63 us (4%)
    ppermute x7, starting transfers between devices, move(): return lax.ppermute(value, 'cond', pairs(z_to, y_to))  14.2 us
    ppermute x7, waiting for transfers between devices, move(): return lax.ppermute(value, 'cond', pairs(z_to, y_to))  7.5 us
    ppermute x2, starting transfers between devices, exchange(): cross_got = lax.ppermute(cross_send, 'blk', cross)  4.6 us
    ppermute x2, waiting for transfers between devices, exchange(): cross_got = lax.ppermute(cross_send, 'blk', cross)  4.31 us
    pallas_call x1, Pallas kernels, body(): call(first_interior_kernel, 'first_interior', [jax.ShapeDtypeStruct((2, J...  2.97 us
    pallas_call x1, Pallas kernels, body(): call(second_boundary_kernel, 'second_boundary', [planes] * 4 + [f32(SLOTS...  1.24 us
    pallas_call x1, Pallas kernels, body(): call(first_boundary_kernel, 'first_boundary', [planes, planes, plane, pla...  1.21 us
    pallas_call x1, Pallas kernels, body(): call(pack_kernel, 'pack_rims', [f32(PLANES, J, K)] * 2, [SMEM] + [HBM] *...  1.05 us
  transfers between devices with their start and end apart: 11, of which 7 were waited for; matrix products, arithmetic and copies ran while one was open for 2% of the time, Pallas kernels for 9%

profile of v3, /device:TPU:32, one launch (start us, length us, event | category | flops | bytes accessed | tf_op | source)
XLA Modules:
  0.0 41.7 jit_solution(3468578796580942363)
XLA Ops:
  0.6 0.0 copy-start.3
  0.6 0.0 copy-start.1
  1.3 1.1 %pack_rims.1 = (f32[76,8,128]{2,1,0:T(8,128)S(1)}, f32[76,8,128]{2,1,0:T(8,128)S(1)}) custom-call(s32[1]{0:T(128)} %copy.39.lengths, f32[1,6,32,8,128]{4,3,2,1,0:T(8,128)} %state.1, f32[1,6,32,8,128]{4,3,2,1,0:T(8,128)} %source.1, f32[1,32,8,128]{3,2,1,0:T(8,128)} %second.1, f32[1,32,8,128]{3,2,1,0:T(8,128)} %fourth.1, f32[1,32,8,128]{3,2,1,0:T(8,128)} %step.1), custom_call_target="tpu_custom_call" | custom-call | tf_op jit(solution)/shard_map/pack_rims/pallas_call | solution.py:317
  2.4 2.3 %collective-permute-start = (f32[76,8,128]{2,1,0:T(8,128)S(1)}, f32[76,8,128]{2,1,0:T(8,128)S(1)}, u32[]{:S(2)}, u32[]{:S(2)}) collective-permute-start(f32[76,8,128]{2,1,0:T(8,128)S(1)} %get-tuple-element.32), channel_id=1, source_target_pairs={{0,224},{32,64},{64,32},{96,128},{128,96},{160,192},{192,160},{224... | collective-permute-start | bytes 933896 | tf_op jit(solution)/shard_map/ppermute | solution.py:312
  4.7 0.0 collective-permute-start.1
  4.7 0.0 copy-done.3
  4.7 0.0 copy-done.1
  4.7 3.0 %first_interior.1 = (s32[2,8,128]{2,1,0:T(8,128)S(1)}, bf16[96,192]{1,0:T(8,128)(2,1)S(1)}, f32[6,44,8,128]{3,2,1,0:T(8,128)S(1)}, f32[6,44,8,128]{3,2,1,0:T(8,1...) custom-call(s32[1]{0:T(128)} %copy.39.lengths, ...), custom_call_target="tpu_custom_call" | custom-call | tf_op jit(solution)/shard_map/first_interior/pallas_call | solution.py:321
  7.7 2.3 %collective-permute-done.cross_got = f32[76,8,128]{2,1,0:T(8,128)S(1)} collective-permute-done((f32[76,8,128]{2,1,0:T(8,128)S(1)}, f32[76,8,128]{2,1,0:T(8,128)S(1)}, u32[]{:S(2)}, u32[]{:S(2)}) %collective-permute-start) | collective-permute-done | bytes 311328 | tf_op jit(solution)/shard_map/ppermute | solution.py:312
  10.0 0.0 collective-permute-done.1.on_got
  10.0 0.0 copy-start
  10.0 1.2 %first_boundary.1 = (f32[6,44,8,128]{3,2,1,0:T(8,128)S(1)}, f32[6,44,8,128]{3,2,1,0:T(8,128)S(1)}, f32[44,8,128]{2,1,0:T(8,128)S(1)}, f32[44,8,128]{2,1,0:T(8,12...) custom-call(s32[1]{0:T(128)} %copy.39.lengths, ...), custom_call_target="tpu_custom_call", output_to_operand_aliasing={{0}: (5, {}), {1}: (6, {}), {2}: (7, {}), {3}: (8, {}), {4}... | custom-call | tf_op jit(solution)/shard_map/first_boundary/pallas_call | solution.py:327
  11.2 2.3 %collective-permute-start.2 = (f32[36,8,128]{2,1,0:T(8,128)S(1)}, f32[36,8,128]{2,1,0:T(8,128)S(1)}, u32[]{:S(2)}, u32[]{:S(2)}) collective-permute-start(f32[36,8,128]{2,1,0:T(8,128)S(1)} %get-tuple-element.42), channel_id=1, source_target_pairs={{0,224},{32,64},{64,32},{96,128},{128,96},{160,192},{192,160},{224... | collective-permute-start | bytes 442376 | tf_op jit(solution)/shard_map/ppermute | solution.py:312
  13.5 0.0 collective-permute-start.3
  14.2 0.0 copy-done
  14.2 0.0 copy-start.2
  14.2 0.9 %second_interior.1 = (f32[6,44,8,128]{3,2,1,0:T(8,128)S(1)}, f32[6,44,8,128]{3,2,1,0:T(8,128)S(1)}, f32[6,44,8,128]{3,2,1,0:T(8,128)S(1)}, f32[32,128]{1,0:T(8,128)S(1)}, f32[32,128]{1,0:T(8,128)S(1)}) custom-call(s32[1]{0:T(128)} %copy.39.lengths, bf16[96,192]{1,0:T(8,128)(2,1)S(1)} %get-tuple-element.31.matrix, ...), custom_call_target="tpu_custom_call" | custom-call | tf_op jit(solution)/shard_map/second_interior/pallas_call | solution.py:334
  15.1 2.0 %collective-permute-done.2.cross_got = f32[36,8,128]{2,1,0:T(8,128)S(1)} collective-permute-done((f32[36,8,128]{2,1,0:T(8,128)S(1)}, f32[36,8,128]{2,1,0:T(8,128)S(1)}, u32[]{:S(2)}, u32[]{:S(2)}) %collective-permute-start.2) | collective-permute-done | bytes 147488 | tf_op jit(solution)/shard_map/ppermute | solution.py:312
  17.1 0.0 collective-permute-done.3.on_got
  17.1 0.0 copy-done.2
  17.1 1.2 %second_boundary.1 = (f32[6,44,8,128]{3,2,1,0:T(8,128)S(1)}, f32[6,44,8,128]{3,2,1,0:T(8,128)S(1)}, f32[6,44,8,128]{3,2,1,0:T(8,128)S(1)}, f32[6,44,8,128]{3,2,1,0:T(8,128)S(1)}, f32[32,128]{1,0:T(8,128)S(1)}) custom-call(s32[1]{0:T(128)} %copy.39.lengths, ...), custom_call_target="tpu_custom_call", output_to_operand_aliasing={{0}: (14, {}), {1}: (15, {}), {2}: (16, {}), {3}: (17, {})} | custom-call | tf_op jit(solution)/shard_map/second_boundary/pallas_call | solution.py:337
  18.4 3.4 %collective-permute-start.4 = (f32[32,128]{1,0:T(8,128)S(1)}, f32[32,128]{1,0:T(8,128)S(1)}, u32[]{:S(2)}, u32[]{:S(2)}) collective-permute-start(f32[32,128]{1,0:T(8,128)S(1)} %get-tuple-element.54), channel_id=1, source_target_pairs={{0,8},{1,9},{2,10},{3,11},{4,12},{5,13},{6,14},{7,15},{8,0},{9,1},... | collective-permute-start | bytes 49160 | tf_op jit(solution)/shard_map/ppermute | solution.py:293
  21.7 0.0 collective-permute-start.5
  21.7 1.5 %collective-permute-start.6 = (f32[32,128]{1,0:T(8,128)S(1)}, f32[32,128]{1,0:T(8,128)S(1)}, u32[]{:S(2)}, u32[]{:S(2)}) collective-permute-start(f32[32,128]{1,0:T(8,128)S(1)} %get-tuple-element.54), channel_id=1, source_target_pairs={{0,4},{1,5},{2,6},{3,7},{4,0},{5,1},{6,2},{7,3},{8,12},{9,13},{10,... | collective-permute-start | bytes 49160 | tf_op jit(solution)/shard_map/ppermute | solution.py:293
  23.3 1.0 %select_bitcast_fusion = f32[1,6,32,8,128]{4,3,2,1,0:T(8,128)} fusion(f32[6,44,8,128]{3,2,1,0:T(8,128)S(1)} %get-tuple-element.55, pred[32]{0:T(512)(128)(4,1)S(1)} %iota_compare_fusion), kind=kLoop, calls=%fused_computation | loop fusion | flops 196608 | bytes 1572896 | tf_op jit(solution)/shard_map/jit(_where)/select_n | solution.py:342
  24.3 0.0 collective-permute-done.4
  24.3 1.2 %collective-permute-done.5 = f32[32,128]{1,0:T(8,128)S(1)} collective-permute-done((f32[32,128]{1,0:T(8,128)S(1)}, f32[32,128]{1,0:T(8,128)S(1)}, u32[]{:S(2)}, u32[]{:S(2)}) %collective-permute-start.5) | collective-permute-done | bytes 16416 | tf_op jit(solution)/shard_map/ppermute | solution.py:293
  25.4 0.0 collective-permute-done.6
  25.5 3.2 %collective-permute-start.7 = (f32[32,128]{1,0:T(8,128)S(1)}, f32[32,128]{1,0:T(8,128)S(1)}, u32[]{:S(2)}, u32[]{:S(2)}) collective-permute-start(f32[32,128]{1,0:T(8,128)S(1)} %add_add_fusion.1), channel_id=1, source_target_pairs={{0,2},{1,3},{2,0},{3,1},{4,6},{5,7},{6,4},{7,5},{8,10},{9,11},{10,... | collective-permute-start | bytes 49160 | tf_op jit(solution)/shard_map/ppermute | solution.py:293
  28.7 0.7 %collective-permute-start.8 = (f32[32,128]{1,0:T(8,128)S(1)}, f32[32,128]{1,0:T(8,128)S(1)}, u32[]{:S(2)}, u32[]{:S(2)}) collective-permute-start(f32[32,128]{1,0:T(8,128)S(1)} %add_add_fusion.1), channel_id=1, source_target_pairs={{0,1},{1,0},{2,3},{3,2},{4,5},{5,4},{6,7},{7,6},{8,9},{9,8},{10,11... | collective-permute-start | bytes 49160 | tf_op jit(solution)/shard_map/ppermute | solution.py:293
  29.4 0.4 collective-permute-start.9
  29.8 1.0 %collective-permute-done.7 = f32[32,128]{1,0:T(8,128)S(1)} collective-permute-done((f32[32,128]{1,0:T(8,128)S(1)}, f32[32,128]{1,0:T(8,128)S(1)}, u32[]{:S(2)}, u32[]{:S(2)}) %collective-permute-start.7) | collective-permute-done | bytes 16416 | tf_op jit(solution)/shard_map/ppermute | solution.py:293
  30.8 1.7 %collective-permute-done.8 = f32[32,128]{1,0:T(8,128)S(1)} collective-permute-done((f32[32,128]{1,0:T(8,128)S(1)}, f32[32,128]{1,0:T(8,128)S(1)}, u32[]{:S(2)}, u32[]{:S(2)}) %collective-permute-start.8) | collective-permute-done | bytes 16416 | tf_op jit(solution)/shard_map/ppermute | solution.py:293
  32.5 1.9 %collective-permute-done.9 = f32[32,128]{1,0:T(8,128)S(1)} collective-permute-done((f32[32,128]{1,0:T(8,128)S(1)}, f32[32,128]{1,0:T(8,128)S(1)}, u32[]{:S(2)}, u32[]{:S(2)}) %collective-permute-start.9) | collective-permute-done | bytes 16416 | tf_op jit(solution)/shard_map/ppermute | solution.py:293
  34.4 5.0 %collective-permute-start.10 = (f32[32,128]{1,0:T(8,128)S(1)}, f32[32,128]{1,0:T(8,128)S(1)}, u32[]{:S(2)}, u32[]{:S(2)}) collective-permute-start(f32[32,128]{1,0:T(8,128)S(1)} %add_add_fusion), channel_id=1, source_target_pairs={{0,28},{1,29},{2,30},{3,31},{4,24},{5,25},{6,26},{7,27},{8,20},{9,... | collective-permute-start | bytes 49160 | tf_op jit(solution)/shard_map/ppermute | solution.py:293
  39.4 1.7 %collective-permute-done.10 = f32[32,128]{1,0:T(8,128)S(1)} collective-permute-done((f32[32,128]{1,0:T(8,128)S(1)}, f32[32,128]{1,0:T(8,128)S(1)}, u32[]{:S(2)}, u32[]{:S(2)}) %collective-permute-start.10) | collective-permute-done | bytes 16416 | tf_op jit(solution)/shard_map/ppermute | solution.py:293
  41.1 0.6 %add.27 = f32[32,128]{1,0:T(8,128)} add(f32[32,128]{1,0:T(8,128)S(1)} %add_add_fusion, f32[32,128]{1,0:T(8,128)S(1)} %collective-permute-done.10) | non-fusion elementwise | flops 4096 | bytes 49152 | tf_op jit(solution)/shard_map/add | solution.py:302
  (4 shorter events, 0.0 us)
Async XLA Ops:
  0.6 4.1 %copy-start.3 = (f32[1,2,6,6]{3,1,2,0:T(2,128)S(1)}, f32[1,2,6,6]{3,1,2,0:T(2,128)}, u32[]{:S(2)}) copy-start(f32[1,2,6,6]{3,1,2,0:T(2,128)} %param.16) | copy-start | bytes 868
  0.6 4.1 %copy-start.1 = (s32[1,2,128,128]{3,2,1,0:T(8,128)S(1)}, s32[1,2,128,128]{3,2,1,0:T(8,128)}, u32[]{:S(2)}) copy-start(s32[1,2,128,128]{3,2,1,0:T(8,128)} %perm.1) | copy-start | bytes 393220
  2.4 7.6 %collective-permute-start = (f32[76,8,128]{2,1,0:T(8,128)S(1)}, f32[76,8,128]{2,1,0:T(8,128)S(1)}, u32[]{:S(2)}, u32[]{:S(2)}) collective-permute-start(f32[76,8,128]{2,1,0:T(8,128)S(1)} %get-tuple-element.32), channel_id=1, source_target_pairs={{0,224},{32,64},{64,32},{96,128},{128,96},{160,192},{192,160},{224... | collective-permute-start | bytes 933896 | tf_op jit(solution)/shard_map/ppermute | solution.py:312
  4.7 5.3 %collective-permute-start.1 = (f32[76,8,128]{2,1,0:T(8,128)S(1)}, f32[76,8,128]{2,1,0:T(8,128)S(1)}, u32[]{:S(2)}, u32[]{:S(2)}) collective-permute-start(f32[76,8,128]{2,1,0:T(8,128)S(1)} %get-tuple-element.33), channel_id=1, source_target_pairs={{0,32},{32,0},{64,96},{96,64},{128,160},{160,128},{192,224},{224,1... | collective-permute-start | bytes 933896 | tf_op jit(solution)/shard_map/ppermute | solution.py:313
  10.0 4.2 %copy-start = (f32[1,6,32,128]{3,2,1,0:T(8,128)S(1)}, f32[1,6,32,128]{3,2,1,0:T(8,128)}, u32[]{:S(2)}) copy-start(f32[1,6,32,128]{3,2,1,0:T(8,128)} %wall_grad.3) | copy-start | bytes 294916
  11.2 5.9 %collective-permute-start.2 = (f32[36,8,128]{2,1,0:T(8,128)S(1)}, f32[36,8,128]{2,1,0:T(8,128)S(1)}, u32[]{:S(2)}, u32[]{:S(2)}) collective-permute-start(f32[36,8,128]{2,1,0:T(8,128)S(1)} %get-tuple-element.42), channel_id=1, source_target_pairs={{0,224},{32,64},{64,32},{96,128},{128,96},{160,192},{192,160},{224... | collective-permute-start | bytes 442376 | tf_op jit(solution)/shard_map/ppermute | solution.py:312
  13.5 3.6 %collective-permute-start.3 = (f32[36,8,128]{2,1,0:T(8,128)S(1)}, f32[36,8,128]{2,1,0:T(8,128)S(1)}, u32[]{:S(2)}, u32[]{:S(2)}) collective-permute-start(f32[36,8,128]{2,1,0:T(8,128)S(1)} %get-tuple-element.43), channel_id=1, source_target_pairs={{0,32},{32,0},{64,96},{96,64},{128,160},{160,128},{192,224},{224,1... | collective-permute-start | bytes 442376 | tf_op jit(solution)/shard_map/ppermute | solution.py:313
  14.2 2.9 %copy-start.2 = (s32[32,128]{1,0:T(8,128)S(1)}, s32[32,128]{1,0:T(8,128)}, u32[]{:S(2)}) copy-start(s32[32,128]{1,0:T(8,128)} %wall_mask.1) | copy-start | bytes 49156
  18.4 5.9 %collective-permute-start.4 = (f32[32,128]{1,0:T(8,128)S(1)}, f32[32,128]{1,0:T(8,128)S(1)}, u32[]{:S(2)}, u32[]{:S(2)}) collective-permute-start(f32[32,128]{1,0:T(8,128)S(1)} %get-tuple-element.54), channel_id=1, source_target_pairs={{0,8},{1,9},{2,10},{3,11},{4,12},{5,13},{6,14},{7,15},{8,0},{9,1},... | collective-permute-start | bytes 49160 | tf_op jit(solution)/shard_map/ppermute | solution.py:293
  21.7 3.7 %collective-permute-start.5 = (f32[32,128]{1,0:T(8,128)S(1)}, f32[32,128]{1,0:T(8,128)S(1)}, u32[]{:S(2)}, u32[]{:S(2)}) collective-permute-start(f32[32,128]{1,0:T(8,128)S(1)} %get-tuple-element.54), channel_id=1, source_target_pairs={{0,12},{1,13},{2,14},{3,15},{4,8},{5,9},{6,10},{7,11},{8,4},{9,5},... | collective-permute-start | bytes 49160 | tf_op jit(solution)/shard_map/ppermute | solution.py:293
  21.7 3.7 %collective-permute-start.6 = (f32[32,128]{1,0:T(8,128)S(1)}, f32[32,128]{1,0:T(8,128)S(1)}, u32[]{:S(2)}, u32[]{:S(2)}) collective-permute-start(f32[32,128]{1,0:T(8,128)S(1)} %get-tuple-element.54), channel_id=1, source_target_pairs={{0,4},{1,5},{2,6},{3,7},{4,0},{5,1},{6,2},{7,3},{8,12},{9,13},{10,... | collective-permute-start | bytes 49160 | tf_op jit(solution)/shard_map/ppermute | solution.py:293
  25.5 5.3 %collective-permute-start.7 = (f32[32,128]{1,0:T(8,128)S(1)}, f32[32,128]{1,0:T(8,128)S(1)}, u32[]{:S(2)}, u32[]{:S(2)}) collective-permute-start(f32[32,128]{1,0:T(8,128)S(1)} %add_add_fusion.1), channel_id=1, source_target_pairs={{0,2},{1,3},{2,0},{3,1},{4,6},{5,7},{6,4},{7,5},{8,10},{9,11},{10,... | collective-permute-start | bytes 49160 | tf_op jit(solution)/shard_map/ppermute | solution.py:293
  28.7 3.7 %collective-permute-start.8 = (f32[32,128]{1,0:T(8,128)S(1)}, f32[32,128]{1,0:T(8,128)S(1)}, u32[]{:S(2)}, u32[]{:S(2)}) collective-permute-start(f32[32,128]{1,0:T(8,128)S(1)} %add_add_fusion.1), channel_id=1, source_target_pairs={{0,1},{1,0},{2,3},{3,2},{4,5},{5,4},{6,7},{7,6},{8,9},{9,8},{10,11... | collective-permute-start | bytes 49160 | tf_op jit(solution)/shard_map/ppermute | solution.py:293
  29.4 4.9 %collective-permute-start.9 = (f32[32,128]{1,0:T(8,128)S(1)}, f32[32,128]{1,0:T(8,128)S(1)}, u32[]{:S(2)}, u32[]{:S(2)}) collective-permute-start(f32[32,128]{1,0:T(8,128)S(1)} %add_add_fusion.1), channel_id=1, source_target_pairs={{0,3},{1,2},{2,1},{3,0},{4,7},{5,6},{6,5},{7,4},{8,11},{9,10},{10,... | collective-permute-start | bytes 49160 | tf_op jit(solution)/shard_map/ppermute | solution.py:293
  34.4 6.7 %collective-permute-start.10 = (f32[32,128]{1,0:T(8,128)S(1)}, f32[32,128]{1,0:T(8,128)S(1)}, u32[]{:S(2)}, u32[]{:S(2)}) collective-permute-start(f32[32,128]{1,0:T(8,128)S(1)} %add_add_fusion), channel_id=1, source_target_pairs={{0,28},{1,29},{2,30},{3,31},{4,24},{5,25},{6,26},{7,27},{8,20},{9,... | collective-permute-start | bytes 49160 | tf_op jit(solution)/shard_map/ppermute | solution.py:293

commit v4 on v3

--- a/solution.py
+++ b/solution.py
@@ -299,7 +299,8 @@
     value = value + move(value, lambda z: z ^ 2, same) + move(value, lambda z: z ^ 3, same) + move(value, lambda z: z ^ 1, same)
     value, adjoint = lax.optimization_barrier((value, adjoint))
     value = value + move(value, same, lambda y: y ^ 2) + move(value, same, lambda y: y ^ 1) + move(value, same, lambda y: y ^ 3)
-    value = value + move(value, lambda z: 7 - z, same)
+    far = {0: 7, 7: 0, 1: 4, 4: 1, 2: 5, 5: 2, 3: 6, 6: 3}
+    value = value + move(value, lambda z: far[z], same)
     return adjoint, value
 
 

time: 41.9 us -> 42.8 us (1.021)
  starting transfers between devices: 18.9 us -> 19.7 us
  Pallas kernels: 7.36 us -> 7.89 us
  waiting for transfers between devices: 11.8 us -> 11.3 us
    ppermute x7, starting transfers between devices: 14.2 us -> 15.2 us  [move(): return lax.ppermute(value, 'cond', pairs(z_to, y_to))]
    ppermute x2, waiting for transfers between devices: 4.31 us -> 3.78 us  [exchange(): cross_got = lax.ppermute(cross_send, 'blk', cross)]
  transfers between devices with their start and end apart: 11 -> 11, of which waited for: 7 -> 7; matrix products, arithmetic and copies ran while one was open for 2% -> 2% of each run, Pallas kernels for 9% -> 10%
where the time goes in v4:
time: 42.8 us; the launch traced here: 42.6 us
  starting transfers between devices  19.7 us (46%)
  waiting for transfers between devices  11.3 us (26%)
  Pallas kernels  7.89 us (18%)
  between operations  2.05 us (5%)
  other arithmetic  1.63 us (4%)
    ppermute x7, starting transfers between devices, move(): return lax.ppermute(value, 'cond', pairs(z_to, y_to))  15.2 us
    ppermute x7, waiting for transfers between devices, move(): return lax.ppermute(value, 'cond', pairs(z_to, y_to))  7.5 us
    ppermute x2, starting transfers between devices, exchange(): cross_got = lax.ppermute(cross_send, 'blk', cross)  4.53 us
    ppermute x2, waiting for transfers between devices, exchange(): cross_got = lax.ppermute(cross_send, 'blk', cross)  3.78 us
    pallas_call x1, Pallas kernels, body(): call(first_interior_kernel, 'first_interior', [jax.ShapeDtypeStruct((2, J...  3.27 us
    pallas_call x1, Pallas kernels, body(): call(second_boundary_kernel, 'second_boundary', [planes] * 4 + [f32(SLOTS...  1.2 us
    pallas_call x1, Pallas kernels, body(): call(first_boundary_kernel, 'first_boundary', [planes, planes, plane, pla...  1.18 us
    pallas_call x1, Pallas kernels, body(): call(second_interior_kernel, 'second_interior', [planes] * 3 + [f32(SLOTS...  1.18 us
  transfers between devices with their start and end apart: 11, of which 7 were waited for; matrix products, arithmetic and copies ran while one was open for 2% of the time, Pallas kernels for 10%

profile of v4, /device:TPU:32, one launch (start us, length us, event | category | flops | bytes accessed | tf_op | source)
XLA Modules:
  0.0 42.6 jit_solution(7003000599131639677)
XLA Ops:
  0.6 0.0 copy-start.3
  0.6 0.0 copy-start.1
  1.3 1.1 %pack_rims.1 = (f32[76,8,128]{2,1,0:T(8,128)S(1)}, f32[76,8,128]{2,1,0:T(8,128)S(1)}) custom-call(s32[1]{0:T(128)} %copy.39.lengths, f32[1,6,32,8,128]{4,3,2,1,0:T(8,128)} %state.1, f32[1,6,32,8,128]{4,3,2,1,0:T(8,128)} %source.1, f32[1,32,8,128]{3,2,1,0:T(8,128)} %second.1, f32[1,32,8,128]{3,2,1,0:T(8,128)} %fourth.1, f32[1,32,8,128]{3,2,1,0:T(8,128)} %step.1), custom_call_target="tpu_custom_call" | custom-call | tf_op jit(solution)/shard_map/pack_rims/pallas_call | solution.py:318
  2.4 2.3 %collective-permute-start = (f32[76,8,128]{2,1,0:T(8,128)S(1)}, f32[76,8,128]{2,1,0:T(8,128)S(1)}, u32[]{:S(2)}, u32[]{:S(2)}) collective-permute-start(f32[76,8,128]{2,1,0:T(8,128)S(1)} %get-tuple-element.32), channel_id=1, source_target_pairs={{0,224},{32,64},{64,32},{96,128},{128,96},{160,192},{192,160},{224... | collective-permute-start | bytes 933896 | tf_op jit(solution)/shard_map/ppermute | solution.py:313
  4.7 0.0 collective-permute-start.1
  4.7 0.0 copy-done.3
  4.7 0.0 copy-done.1
  4.7 3.3 %first_interior.1 = (s32[2,8,128]{2,1,0:T(8,128)S(1)}, bf16[96,192]{1,0:T(8,128)(2,1)S(1)}, f32[6,44,8,128]{3,2,1,0:T(8,128)S(1)}, f32[6,44,8,128]{3,2,1,0:T(8,1...) custom-call(s32[1]{0:T(128)} %copy.39.lengths, ...), custom_call_target="tpu_custom_call" | custom-call | tf_op jit(solution)/shard_map/first_interior/pallas_call | solution.py:322
  7.9 2.1 %collective-permute-done.cross_got = f32[76,8,128]{2,1,0:T(8,128)S(1)} collective-permute-done((f32[76,8,128]{2,1,0:T(8,128)S(1)}, f32[76,8,128]{2,1,0:T(8,128)S(1)}, u32[]{:S(2)}, u32[]{:S(2)}) %collective-permute-start) | collective-permute-done | bytes 311328 | tf_op jit(solution)/shard_map/ppermute | solution.py:313
  10.0 0.0 collective-permute-done.1.on_got
  10.0 0.0 copy-start
  10.0 1.2 %first_boundary.1 = (f32[6,44,8,128]{3,2,1,0:T(8,128)S(1)}, f32[6,44,8,128]{3,2,1,0:T(8,128)S(1)}, f32[44,8,128]{2,1,0:T(8,128)S(1)}, f32[44,8,128]{2,1,0:T(8,12...) custom-call(s32[1]{0:T(128)} %copy.39.lengths, ...), custom_call_target="tpu_custom_call", output_to_operand_aliasing={{0}: (5, {}), {1}: (6, {}), {2}: (7, {}), {3}: (8, {}), {4}... | custom-call | tf_op jit(solution)/shard_map/first_boundary/pallas_call | solution.py:328
  11.2 2.3 %collective-permute-start.2 = (f32[36,8,128]{2,1,0:T(8,128)S(1)}, f32[36,8,128]{2,1,0:T(8,128)S(1)}, u32[]{:S(2)}, u32[]{:S(2)}) collective-permute-start(f32[36,8,128]{2,1,0:T(8,128)S(1)} %get-tuple-element.42), channel_id=1, source_target_pairs={{0,224},{32,64},{64,32},{96,128},{128,96},{160,192},{192,160},{224... | collective-permute-start | bytes 442376 | tf_op jit(solution)/shard_map/ppermute | solution.py:313
  13.5 0.0 collective-permute-start.3
  14.1 0.0 copy-done
  14.2 0.0 copy-start.2
  14.2 1.2 %second_interior.1 = (f32[6,44,8,128]{3,2,1,0:T(8,128)S(1)}, f32[6,44,8,128]{3,2,1,0:T(8,128)S(1)}, f32[6,44,8,128]{3,2,1,0:T(8,128)S(1)}, f32[32,128]{1,0:T(8,128)S(1)}, f32[32,128]{1,0:T(8,128)S(1)}) custom-call(s32[1]{0:T(128)} %copy.39.lengths, bf16[96,192]{1,0:T(8,128)(2,1)S(1)} %get-tuple-element.31.matrix, ...), custom_call_target="tpu_custom_call" | custom-call | tf_op jit(solution)/shard_map/second_interior/pallas_call | solution.py:335
  15.4 1.7 %collective-permute-done.2.cross_got = f32[36,8,128]{2,1,0:T(8,128)S(1)} collective-permute-done((f32[36,8,128]{2,1,0:T(8,128)S(1)}, f32[36,8,128]{2,1,0:T(8,128)S(1)}, u32[]{:S(2)}, u32[]{:S(2)}) %collective-permute-start.2) | collective-permute-done | bytes 147488 | tf_op jit(solution)/shard_map/ppermute | solution.py:313
  17.1 0.0 collective-permute-done.3.on_got
  17.1 0.0 copy-done.2
  17.1 1.2 %second_boundary.1 = (f32[6,44,8,128]{3,2,1,0:T(8,128)S(1)}, f32[6,44,8,128]{3,2,1,0:T(8,128)S(1)}, f32[6,44,8,128]{3,2,1,0:T(8,128)S(1)}, f32[6,44,8,128]{3,2,1,0:T(8,128)S(1)}, f32[32,128]{1,0:T(8,128)S(1)}) custom-call(s32[1]{0:T(128)} %copy.39.lengths, ...), custom_call_target="tpu_custom_call", output_to_operand_aliasing={{0}: (14, {}), {1}: (15, {}), {2}: (16, {}), {3}: (17, {})} | custom-call | tf_op jit(solution)/shard_map/second_boundary/pallas_call | solution.py:338
  18.3 3.4 %collective-permute-start.4 = (f32[32,128]{1,0:T(8,128)S(1)}, f32[32,128]{1,0:T(8,128)S(1)}, u32[]{:S(2)}, u32[]{:S(2)}) collective-permute-start(f32[32,128]{1,0:T(8,128)S(1)} %get-tuple-element.54), channel_id=1, source_target_pairs={{0,8},{1,9},{2,10},{3,11},{4,12},{5,13},{6,14},{7,15},{8,0},{9,1},... | collective-permute-start | bytes 49160 | tf_op jit(solution)/shard_map/ppermute | solution.py:293
  21.6 0.0 collective-permute-start.5
  21.7 1.5 %collective-permute-start.6 = (f32[32,128]{1,0:T(8,128)S(1)}, f32[32,128]{1,0:T(8,128)S(1)}, u32[]{:S(2)}, u32[]{:S(2)}) collective-permute-start(f32[32,128]{1,0:T(8,128)S(1)} %get-tuple-element.54), channel_id=1, source_target_pairs={{0,4},{1,5},{2,6},{3,7},{4,0},{5,1},{6,2},{7,3},{8,12},{9,13},{10,... | collective-permute-start | bytes 49160 | tf_op jit(solution)/shard_map/ppermute | solution.py:293
  23.2 1.0 %select_bitcast_fusion = f32[1,6,32,8,128]{4,3,2,1,0:T(8,128)} fusion(f32[6,44,8,128]{3,2,1,0:T(8,128)S(1)} %get-tuple-element.55, pred[32]{0:T(512)(128)(4,1)S(1)} %iota_compare_fusion), kind=kLoop, calls=%fused_computation | loop fusion | flops 196608 | bytes 1572896 | tf_op jit(solution)/shard_map/jit(_where)/select_n | solution.py:343
  24.2 0.0 collective-permute-done.4
  24.2 1.2 %collective-permute-done.5 = f32[32,128]{1,0:T(8,128)S(1)} collective-permute-done((f32[32,128]{1,0:T(8,128)S(1)}, f32[32,128]{1,0:T(8,128)S(1)}, u32[]{:S(2)}, u32[]{:S(2)}) %collective-permute-start.5) | collective-permute-done | bytes 16416 | tf_op jit(solution)/shard_map/ppermute | solution.py:293
  25.4 0.0 collective-permute-done.6
  25.4 3.3 %collective-permute-start.7 = (f32[32,128]{1,0:T(8,128)S(1)}, f32[32,128]{1,0:T(8,128)S(1)}, u32[]{:S(2)}, u32[]{:S(2)}) collective-permute-start(f32[32,128]{1,0:T(8,128)S(1)} %add_add_fusion.1), channel_id=1, source_target_pairs={{0,2},{1,3},{2,0},{3,1},{4,6},{5,7},{6,4},{7,5},{8,10},{9,11},{10,... | collective-permute-start | bytes 49160 | tf_op jit(solution)/shard_map/ppermute | solution.py:293
  28.7 0.7 %collective-permute-start.8 = (f32[32,128]{1,0:T(8,128)S(1)}, f32[32,128]{1,0:T(8,128)S(1)}, u32[]{:S(2)}, u32[]{:S(2)}) collective-permute-start(f32[32,128]{1,0:T(8,128)S(1)} %add_add_fusion.1), channel_id=1, source_target_pairs={{0,1},{1,0},{2,3},{3,2},{4,5},{5,4},{6,7},{7,6},{8,9},{9,8},{10,11... | collective-permute-start | bytes 49160 | tf_op jit(solution)/shard_map/ppermute | solution.py:293
  29.4 0.4 collective-permute-start.9
  29.7 1.0 %collective-permute-done.7 = f32[32,128]{1,0:T(8,128)S(1)} collective-permute-done((f32[32,128]{1,0:T(8,128)S(1)}, f32[32,128]{1,0:T(8,128)S(1)}, u32[]{:S(2)}, u32[]{:S(2)}) %collective-permute-start.7) | collective-permute-done | bytes 16416 | tf_op jit(solution)/shard_map/ppermute | solution.py:293
  30.7 1.7 %collective-permute-done.8 = f32[32,128]{1,0:T(8,128)S(1)} collective-permute-done((f32[32,128]{1,0:T(8,128)S(1)}, f32[32,128]{1,0:T(8,128)S(1)}, u32[]{:S(2)}, u32[]{:S(2)}) %collective-permute-start.8) | collective-permute-done | bytes 16416 | tf_op jit(solution)/shard_map/ppermute | solution.py:293
  32.4 1.9 %collective-permute-done.9 = f32[32,128]{1,0:T(8,128)S(1)} collective-permute-done((f32[32,128]{1,0:T(8,128)S(1)}, f32[32,128]{1,0:T(8,128)S(1)}, u32[]{:S(2)}, u32[]{:S(2)}) %collective-permute-start.9) | collective-permute-done | bytes 16416 | tf_op jit(solution)/shard_map/ppermute | solution.py:293
  34.3 6.0 %collective-permute-start.10 = (f32[32,128]{1,0:T(8,128)S(1)}, f32[32,128]{1,0:T(8,128)S(1)}, u32[]{:S(2)}, u32[]{:S(2)}) collective-permute-start(f32[32,128]{1,0:T(8,128)S(1)} %add_add_fusion), channel_id=1, source_target_pairs={{0,28},{1,29},{2,30},{3,31},{4,16},{5,17},{6,18},{7,19},{8,20},{9,... | collective-permute-start | bytes 49160 | tf_op jit(solution)/shard_map/ppermute | solution.py:293
  40.3 1.7 %collective-permute-done.10 = f32[32,128]{1,0:T(8,128)S(1)} collective-permute-done((f32[32,128]{1,0:T(8,128)S(1)}, f32[32,128]{1,0:T(8,128)S(1)}, u32[]{:S(2)}, u32[]{:S(2)}) %collective-permute-start.10) | collective-permute-done | bytes 16416 | tf_op jit(solution)/shard_map/ppermute | solution.py:293
  42.0 0.6 %add.27 = f32[32,128]{1,0:T(8,128)} add(f32[32,128]{1,0:T(8,128)S(1)} %add_add_fusion, f32[32,128]{1,0:T(8,128)S(1)} %collective-permute-done.10) | non-fusion elementwise | flops 4096 | bytes 49152 | tf_op jit(solution)/shard_map/add | solution.py:303
  (4 shorter events, 0.0 us)
Async XLA Ops:
  0.6 4.0 %copy-start.3 = (f32[1,2,6,6]{3,1,2,0:T(2,128)S(1)}, f32[1,2,6,6]{3,1,2,0:T(2,128)}, u32[]{:S(2)}) copy-start(f32[1,2,6,6]{3,1,2,0:T(2,128)} %param.16) | copy-start | bytes 868
  0.6 4.0 %copy-start.1 = (s32[1,2,128,128]{3,2,1,0:T(8,128)S(1)}, s32[1,2,128,128]{3,2,1,0:T(8,128)}, u32[]{:S(2)}) copy-start(s32[1,2,128,128]{3,2,1,0:T(8,128)} %perm.1) | copy-start | bytes 393220
  2.4 7.6 %collective-permute-start = (f32[76,8,128]{2,1,0:T(8,128)S(1)}, f32[76,8,128]{2,1,0:T(8,128)S(1)}, u32[]{:S(2)}, u32[]{:S(2)}) collective-permute-start(f32[76,8,128]{2,1,0:T(8,128)S(1)} %get-tuple-element.32), channel_id=1, source_target_pairs={{0,224},{32,64},{64,32},{96,128},{128,96},{160,192},{192,160},{224... | collective-permute-start | bytes 933896 | tf_op jit(solution)/shard_map/ppermute | solution.py:313
  4.7 5.4 %collective-permute-start.1 = (f32[76,8,128]{2,1,0:T(8,128)S(1)}, f32[76,8,128]{2,1,0:T(8,128)S(1)}, u32[]{:S(2)}, u32[]{:S(2)}) collective-permute-start(f32[76,8,128]{2,1,0:T(8,128)S(1)} %get-tuple-element.33), channel_id=1, source_target_pairs={{0,32},{32,0},{64,96},{96,64},{128,160},{160,128},{192,224},{224,1... | collective-permute-start | bytes 933896 | tf_op jit(solution)/shard_map/ppermute | solution.py:314
  10.0 4.1 %copy-start = (f32[1,6,32,128]{3,2,1,0:T(8,128)S(1)}, f32[1,6,32,128]{3,2,1,0:T(8,128)}, u32[]{:S(2)}) copy-start(f32[1,6,32,128]{3,2,1,0:T(8,128)} %wall_grad.3) | copy-start | bytes 294916
  11.2 5.9 %collective-permute-start.2 = (f32[36,8,128]{2,1,0:T(8,128)S(1)}, f32[36,8,128]{2,1,0:T(8,128)S(1)}, u32[]{:S(2)}, u32[]{:S(2)}) collective-permute-start(f32[36,8,128]{2,1,0:T(8,128)S(1)} %get-tuple-element.42), channel_id=1, source_target_pairs={{0,224},{32,64},{64,32},{96,128},{128,96},{160,192},{192,160},{224... | collective-permute-start | bytes 442376 | tf_op jit(solution)/shard_map/ppermute | solution.py:313
  13.5 3.6 %collective-permute-start.3 = (f32[36,8,128]{2,1,0:T(8,128)S(1)}, f32[36,8,128]{2,1,0:T(8,128)S(1)}, u32[]{:S(2)}, u32[]{:S(2)}) collective-permute-start(f32[36,8,128]{2,1,0:T(8,128)S(1)} %get-tuple-element.43), channel_id=1, source_target_pairs={{0,32},{32,0},{64,96},{96,64},{128,160},{160,128},{192,224},{224,1... | collective-permute-start | bytes 442376 | tf_op jit(solution)/shard_map/ppermute | solution.py:314
  14.2 2.9 %copy-start.2 = (s32[32,128]{1,0:T(8,128)S(1)}, s32[32,128]{1,0:T(8,128)}, u32[]{:S(2)}) copy-start(s32[32,128]{1,0:T(8,128)} %wall_mask.1) | copy-start | bytes 49156
  18.3 5.9 %collective-permute-start.4 = (f32[32,128]{1,0:T(8,128)S(1)}, f32[32,128]{1,0:T(8,128)S(1)}, u32[]{:S(2)}, u32[]{:S(2)}) collective-permute-start(f32[32,128]{1,0:T(8,128)S(1)} %get-tuple-element.54), channel_id=1, source_target_pairs={{0,8},{1,9},{2,10},{3,11},{4,12},{5,13},{6,14},{7,15},{8,0},{9,1},... | collective-permute-start | bytes 49160 | tf_op jit(solution)/shard_map/ppermute | solution.py:293
  21.6 3.7 %collective-permute-start.5 = (f32[32,128]{1,0:T(8,128)S(1)}, f32[32,128]{1,0:T(8,128)S(1)}, u32[]{:S(2)}, u32[]{:S(2)}) collective-permute-start(f32[32,128]{1,0:T(8,128)S(1)} %get-tuple-element.54), channel_id=1, source_target_pairs={{0,12},{1,13},{2,14},{3,15},{4,8},{5,9},{6,10},{7,11},{8,4},{9,5},... | collective-permute-start | bytes 49160 | tf_op jit(solution)/shard_map/ppermute | solution.py:293
  21.7 3.7 %collective-permute-start.6 = (f32[32,128]{1,0:T(8,128)S(1)}, f32[32,128]{1,0:T(8,128)S(1)}, u32[]{:S(2)}, u32[]{:S(2)}) collective-permute-start(f32[32,128]{1,0:T(8,128)S(1)} %get-tuple-element.54), channel_id=1, source_target_pairs={{0,4},{1,5},{2,6},{3,7},{4,0},{5,1},{6,2},{7,3},{8,12},{9,13},{10,... | collective-permute-start | bytes 49160 | tf_op jit(solution)/shard_map/ppermute | solution.py:293
  25.4 5.3 %collective-permute-start.7 = (f32[32,128]{1,0:T(8,128)S(1)}, f32[32,128]{1,0:T(8,128)S(1)}, u32[]{:S(2)}, u32[]{:S(2)}) collective-permute-start(f32[32,128]{1,0:T(8,128)S(1)} %add_add_fusion.1), channel_id=1, source_target_pairs={{0,2},{1,3},{2,0},{3,1},{4,6},{5,7},{6,4},{7,5},{8,10},{9,11},{10,... | collective-permute-start | bytes 49160 | tf_op jit(solution)/shard_map/ppermute | solution.py:293
  28.7 3.7 %collective-permute-start.8 = (f32[32,128]{1,0:T(8,128)S(1)}, f32[32,128]{1,0:T(8,128)S(1)}, u32[]{:S(2)}, u32[]{:S(2)}) collective-permute-start(f32[32,128]{1,0:T(8,128)S(1)} %add_add_fusion.1), channel_id=1, source_target_pairs={{0,1},{1,0},{2,3},{3,2},{4,5},{5,4},{6,7},{7,6},{8,9},{9,8},{10,11... | collective-permute-start | bytes 49160 | tf_op jit(solution)/shard_map/ppermute | solution.py:293
  29.4 4.9 %collective-permute-start.9 = (f32[32,128]{1,0:T(8,128)S(1)}, f32[32,128]{1,0:T(8,128)S(1)}, u32[]{:S(2)}, u32[]{:S(2)}) collective-permute-start(f32[32,128]{1,0:T(8,128)S(1)} %add_add_fusion.1), channel_id=1, source_target_pairs={{0,3},{1,2},{2,1},{3,0},{4,7},{5,6},{6,5},{7,4},{8,11},{9,10},{10,... | collective-permute-start | bytes 49160 | tf_op jit(solution)/shard_map/ppermute | solution.py:293
  34.3 7.7 %collective-permute-start.10 = (f32[32,128]{1,0:T(8,128)S(1)}, f32[32,128]{1,0:T(8,128)S(1)}, u32[]{:S(2)}, u32[]{:S(2)}) collective-permute-start(f32[32,128]{1,0:T(8,128)S(1)} %add_add_fusion), channel_id=1, source_target_pairs={{0,28},{1,29},{2,30},{3,31},{4,16},{5,17},{6,18},{7,19},{8,20},{9,... | collective-permute-start | bytes 49160 | tf_op jit(solution)/shard_map/ppermute | solution.py:293
